TPU v7x, 128 devices: a whole 4x4x4 slice. The times are simulated.
128 devices in a mesh: group: 8 (over y_hi, z), dp: 16 (over x, y_lo, core).
Axes of the slice: x: 4, y: 4 (y_hi: 2, y_lo: 2; y = y_hi * 2 + y_lo), z: 4, core: 2. Of those that a mesh axis runs over, the one named last changes fastest.
Arguments:
- tokens: float32 [128, 577, 384], P(('group', 'dp')), may hold values from -6 to 6
- cotangent: float32 [128, 577, 384], P(('group', 'dp')), may hold values from -6 to 6
- live: int32 [128], P(('group', 'dp')), may hold values from 0 to 1, as said below
- slot_of: int32 [8], replicated, may hold values from 0 to 7, as said below
- weights: float32 [8, 384, 1536], P('group', None, 'dp'), as said below
- momentum: float32 [8, 384, 1536], P('group', None, 'dp'), as said below
- vec: float32 [24, 384], P('group', 'dp')
- vec_first: float32 [24, 384], P('group', 'dp')
- vec_second: float32 [24, 384], P('group', 'dp'), as said below
Outputs:
- block_out: float32 [128, 577, 384], P(('group', 'dp'))
- token_grad: float32 [128, 577, 384], P(('group', 'dp'))
- weight_grad: float32 [8, 384, 1536], P('group', None, 'dp')
- new_momentum: float32 [8, 384, 1536], P('group', None, 'dp')
- new_weights: float32 [8, 384, 1536], P('group', None, 'dp')
- first_new: float32 [24, 384], P('group', 'dp')
- second_new: float32 [24, 384], P('group', 'dp')
- vec_new: float32 [24, 384], P('group', 'dp')
Inputs may be any that keep to these rules, and one draw needn't show every extreme that they name: `live`: 1 where the device's slot holds an image, 0 where it is empty; every draw has full and empty slots. A permutation: matrix m lies in slot slot_of[m]; slot q lies on group index q. `weights`: slot q holds the matrix m with slot_of[m] = q in its first n(m) columns and zeros beyond. `momentum`: laid out like weights, zeros beyond n(m) columns. `vec_second`: positive.
All inputs are finite; a program needn't handle non-finite values.
Results may differ from a plain program's by a relative error of at most 0.02.
The roundings to bfloat16 on the way count: a program that leaves them out, or rounds other values in their place, can miss the bound.
Values may be sent and summed in bfloat16 or wider, within the bound.
No kernel may reach another device: no remote copies, remote signals or barrier semaphores. Data moves between devices by JAX's collectives and lax.ppermute only.
A program may use at most 192 MiB of HBM per device.

v0:
```python
import jax
import jax.numpy as jnp
from jax import lax
from jax.sharding import PartitionSpec as P

HEADS = 6
FF = 1536
LAYERS = 2
NEWTON_STEPS = 5
STEP = 10
MATS = 8
VROWS = 24


norm_eps = 1e-06
ortho_eps = 1e-07
coef_a = 3.4445
coef_b = -4.775
coef_c = 2.0315
momentum_keep = 0.95
muon_rate = 0.25
muon_decay = 0.01
muon_shape = 0.5
adam_rate = 0.4
first_keep = 0.9
second_keep = 0.999
adam_eps = 1e-08
highest = lax.Precision.HIGHEST
half_root = 0.7071067811865476
density = 0.3989422804014327


def normalize(values):
    center = values - jnp.mean(values, -1, keepdims=True)
    inv_std = lax.rsqrt(jnp.mean(center * center, -1, keepdims=True) + norm_eps)
    return (center * inv_std, inv_std)


def norm_back(upstream, normed, inv_std, gain):
    scaled = upstream * gain
    return inv_std * (
        scaled
        - jnp.mean(scaled, -1, keepdims=True)
        - normed * jnp.mean(scaled * normed, -1, keepdims=True)
    )


def gelu_slope(values):
    return (
        0.5 * (1.0 + lax.erf(values * half_root))
        + values * jnp.exp(-0.5 * values * values) * density
    )


def row_contract(left_op, right_op):
    return lax.dot_general(
        left_op, right_op, (((0,), (0,)), ((), ())), preferred_element_type=jnp.float32
    )


def col_contract(left_op, right_op):
    return lax.dot_general(
        left_op, right_op, (((1,), (1,)), ((), ())), preferred_element_type=jnp.float32
    )


def split_heads(packed, head_count):
    length, triple = packed.shape
    features = triple // 3
    head_size = features // head_count
    pieces = [
        packed[:, slot_at * features : (slot_at + 1) * features].reshape(
            length, head_count, head_size
        )
        for slot_at in range(3)
    ]
    return (pieces[0], pieces[1], pieces[2])


def layer_forward(inputs, w_qkv, w_out, w_up, w_down, vec_rows, head_count):
    length, features = inputs.shape
    head_size = features // head_count
    normed_one, inv_one = normalize(inputs)
    normed_low = (normed_one * vec_rows[0] + vec_rows[1]).astype(jnp.bfloat16)
    qkv_bias = jnp.concatenate([vec_rows[2], jnp.zeros_like(vec_rows[2]), vec_rows[3]])
    qkv_low = (jnp.dot(normed_low, w_qkv, preferred_element_type=jnp.float32) + qkv_bias).astype(
        jnp.bfloat16
    )
    queries, key_heads, value_heads = split_heads(qkv_low, head_count)
    scores = jnp.einsum(
        "qhd,khd->hqk", queries, key_heads, preferred_element_type=jnp.float32
    ) * head_size ** (-0.5)
    row_max = jnp.max(scores, -1, keepdims=True)
    exponent = jnp.exp(scores - row_max)
    row_sum = jnp.sum(exponent, -1, keepdims=True)
    log_total = row_max + jnp.log(row_sum)
    prob_low = (exponent / row_sum).astype(jnp.bfloat16)
    attended = jnp.einsum("hqk,khd->qhd", prob_low, value_heads, preferred_element_type=jnp.float32)
    attn_low = attended.reshape(length, features).astype(jnp.bfloat16)
    middle = inputs + (jnp.dot(attn_low, w_out, preferred_element_type=jnp.float32) + vec_rows[4])
    normed_two, inv_two = normalize(middle)
    hidden_low = (normed_two * vec_rows[5] + vec_rows[6]).astype(jnp.bfloat16)
    hidden = jnp.dot(hidden_low, w_up, preferred_element_type=jnp.float32) + vec_rows[8:].reshape(
        -1
    )
    active_low = jax.nn.gelu(hidden, approximate=False).astype(jnp.bfloat16)
    result = middle + (col_contract(active_low, w_down) + vec_rows[7])
    stored = (
        normed_one,
        inv_one,
        normed_low,
        qkv_low,
        log_total,
        attn_low,
        normed_two,
        inv_two,
        hidden_low,
        hidden,
        active_low,
    )
    return (result, stored)


def layer_backward(upstream, w_qkv, w_out, w_up, w_down, vec_rows, stored, head_count):
    (
        normed_one,
        inv_one,
        normed_low,
        qkv_low,
        log_total,
        attn_low,
        normed_two,
        inv_two,
        hidden_low,
        hidden,
        active_low,
    ) = stored
    length, features = upstream.shape
    head_size = features // head_count
    down_low = upstream.astype(jnp.bfloat16)
    grad_down = row_contract(down_low, active_low)
    up_low = (
        jnp.dot(down_low, w_down, preferred_element_type=jnp.float32) * gelu_slope(hidden)
    ).astype(jnp.bfloat16)
    grad_up = row_contract(hidden_low, up_low)
    back_hidden = col_contract(up_low, w_up)
    middle_grad = upstream + norm_back(back_hidden, normed_two, inv_two, vec_rows[5])
    out_low = middle_grad.astype(jnp.bfloat16)
    grad_out = row_contract(attn_low, out_low)
    attn_grad = (
        col_contract(out_low, w_out).astype(jnp.bfloat16).reshape(length, head_count, head_size)
    )
    queries, key_heads, value_heads = split_heads(qkv_low, head_count)
    scores = jnp.einsum(
        "qhd,khd->hqk", queries, key_heads, preferred_element_type=jnp.float32
    ) * head_size ** (-0.5)
    prob_rows = jnp.exp(scores - log_total)
    value_grad = jnp.einsum(
        "hqk,qhd->khd",
        prob_rows.astype(jnp.bfloat16),
        attn_grad,
        preferred_element_type=jnp.float32,
    )
    prob_grad = jnp.einsum(
        "qhd,khd->hqk", attn_grad, value_heads, preferred_element_type=jnp.float32
    )
    score_low = (
        prob_rows * (prob_grad - jnp.sum(prob_grad * prob_rows, -1, keepdims=True))
    ).astype(jnp.bfloat16)
    query_grad = jnp.einsum(
        "hqk,khd->qhd", score_low, key_heads, preferred_element_type=jnp.float32
    ) * head_size ** (-0.5)
    key_grad = jnp.einsum(
        "hqk,qhd->khd", score_low, queries, preferred_element_type=jnp.float32
    ) * head_size ** (-0.5)
    qkv_grad = jnp.concatenate(
        [
            query_grad.reshape(length, features),
            key_grad.reshape(length, features),
            value_grad.reshape(length, features),
        ],
        1,
    ).astype(jnp.bfloat16)
    grad_qkv = row_contract(normed_low, qkv_grad)
    back_normed = col_contract(qkv_grad, w_qkv)
    input_grad = middle_grad + norm_back(back_normed, normed_one, inv_one, vec_rows[0])
    qkv_sum = jnp.sum(qkv_grad.astype(jnp.float32), 0)
    vec_grad = jnp.concatenate(
        [
            jnp.stack(
                [
                    jnp.sum(back_normed * normed_one, 0),
                    jnp.sum(back_normed, 0),
                    qkv_sum[:features],
                    qkv_sum[2 * features :],
                    jnp.sum(out_low.astype(jnp.float32), 0),
                    jnp.sum(back_hidden * normed_two, 0),
                    jnp.sum(back_hidden, 0),
                    jnp.sum(down_low.astype(jnp.float32), 0),
                ]
            ),
            jnp.sum(up_low.astype(jnp.float32), 0).reshape(-1, features),
        ],
        0,
    )
    return (input_grad, (grad_qkv, grad_out, grad_up, grad_down), vec_grad)


def orthogonalize(moment):
    norm_value = jnp.sqrt(jnp.sum(moment * moment, axis=(1, 2), keepdims=True))
    current = moment / (norm_value + ortho_eps)
    for iteration in range(NEWTON_STEPS):
        gram_sum = jnp.einsum("sdc,sec->sde", current, current, precision=highest)
        polynomial = coef_b * gram_sum + coef_c * jnp.einsum(
            "sde,sef->sdf", gram_sum, gram_sum, precision=highest
        )
        current = coef_a * current + jnp.einsum(
            "sde,sec->sdc", polynomial, current, precision=highest
        )
    return current


def on_device(tokens, cotangent, live, slot_of, weights, momentum, vec, vec_first, vec_second):
    group_n = lax.axis_size("group")
    data_n = lax.axis_size("dp")
    slots_here, features, columns = weights.shape
    vec_here, vec_cols = vec.shape
    widths = [3 * features, features, FF, FF]
    per_layer = VROWS // LAYERS
    owner_mats, owner_vec = (
        lax.all_gather(weights.astype(jnp.bfloat16), "group", axis=0, tiled=True),
        lax.all_gather(vec.astype(jnp.bfloat16), "group", axis=0, tiled=True),
    )
    all_weights, all_vec = (
        lax.all_gather(owner_mats, "dp", axis=2, tiled=True),
        lax.all_gather(owner_vec, "dp", axis=1, tiled=True),
    )
    vec_full = all_vec.astype(jnp.float32)
    matrices = [
        lax.dynamic_index_in_dim(all_weights, slot_of[mat_index], 0, keepdims=False)[
            :, : widths[mat_index % 4]
        ]
        for mat_index in range(MATS)
    ]
    stream = tokens[0]
    memory = []
    for layer_at in range(LAYERS):
        layer_mats = matrices[4 * layer_at : 4 * layer_at + 4]
        vec_rows = vec_full[layer_at * per_layer : (layer_at + 1) * per_layer]
        stream, stored = layer_forward(
            stream, layer_mats[0], layer_mats[1], layer_mats[2], layer_mats[3], vec_rows, HEADS
        )
        memory.append(stored)
    upstream = cotangent[0] * live.astype(jnp.float32)[0]
    mat_grads = [None] * MATS
    vec_grads = [None] * LAYERS
    for layer_at in range(LAYERS - 1, -1, -1):
        layer_mats = matrices[4 * layer_at : 4 * layer_at + 4]
        vec_rows = vec_full[layer_at * per_layer : (layer_at + 1) * per_layer]
        upstream, four_grads, vec_grads[layer_at] = layer_backward(
            upstream,
            layer_mats[0],
            layer_mats[1],
            layer_mats[2],
            layer_mats[3],
            vec_rows,
            memory[layer_at],
            HEADS,
        )
        for member in range(4):
            piece_grad = four_grads[member]
            mat_grads[4 * layer_at + member] = jnp.pad(
                piece_grad, ((0, 0), (0, FF - piece_grad.shape[1]))
            )
    stacked = jnp.stack(mat_grads)
    vec_all = jnp.concatenate(vec_grads, 0)
    slot_ids = lax.iota(jnp.int32, MATS)
    slot_match = slot_of[None, :] == slot_ids[:, None]
    mat_of = jnp.sum(jnp.where(slot_match, slot_ids[None, :], 0), 1)
    by_slot = jnp.take(stacked, mat_of, axis=0)
    data_at = lax.axis_index("dp")
    spread_mats = by_slot.reshape(group_n, slots_here, features, data_n, columns).transpose(
        0, 3, 1, 2, 4
    )
    spread_vec = vec_all.reshape(group_n, vec_here, data_n, vec_cols).transpose(0, 2, 1, 3)
    shard_grad, shard_vec = (
        lax.psum_scatter(
            spread_mats.reshape(-1, features, columns),
            ("group", "dp"),
            scatter_dimension=0,
            tiled=True,
        ),
        lax.psum_scatter(
            spread_vec.reshape(-1, vec_cols), ("group", "dp"), scatter_dimension=0, tiled=True
        ),
    )
    new_moment = momentum_keep * momentum + shard_grad
    whole = lax.all_gather(new_moment.astype(jnp.bfloat16), "dp", axis=2, tiled=True).astype(
        new_moment.dtype
    )
    ortho = lax.dynamic_slice_in_dim(orthogonalize(whole), data_at * columns, columns, 2)
    my_slots = lax.axis_index("group") * slots_here + lax.iota(jnp.int32, slots_here)
    width_row = jnp.array(widths * LAYERS, jnp.float32)
    mine_match = slot_of[None, :] == my_slots[:, None]
    slot_width = jnp.sum(jnp.where(mine_match, width_row[None, :], 0.0), 1)
    step_scale = (muon_rate * muon_shape * jnp.sqrt(slot_width))[:, None, None]
    new_weights = weights * (1.0 - muon_rate * muon_decay) - step_scale * ortho
    first_new = first_keep * vec_first + (1.0 - first_keep) * shard_vec
    second_new = second_keep * vec_second + (1.0 - second_keep) * shard_vec * shard_vec
    vec_new = vec - adam_rate * (
        first_new
        / (1.0 - first_keep**STEP)
        / (jnp.sqrt(second_new / (1.0 - second_keep**STEP)) + adam_eps)
    )
    return (
        stream[None],
        upstream[None],
        shard_grad,
        new_moment,
        new_weights,
        first_new,
        second_new,
        vec_new,
    )


def solution(mesh):
    placed = (
        P(("group", "dp"), None, None),
        P(("group", "dp"), None, None),
        P(("group", "dp")),
        P(),
        P("group", None, "dp"),
        P("group", None, "dp"),
        P("group", "dp"),
        P("group", "dp"),
        P("group", "dp"),
    )
    return jax.shard_map(
        on_device,
        mesh=mesh,
        in_specs=placed,
        out_specs=(
            P(("group", "dp"), None, None),
            P(("group", "dp"), None, None),
            P("group", None, "dp"),
            P("group", None, "dp"),
            P("group", None, "dp"),
            P("group", "dp"),
            P("group", "dp"),
            P("group", "dp"),
        ),
        check_vma=False,
    )
```

profile of v0, /device:TPU:1, one launch (start us, length us, event | category | flops | bytes accessed | tf_op | source)
XLA Modules:
  0.0 1122.5 jit_solution(13949052626289216004)
XLA Ops:
  8.2 33.6 %all_gather.17 = bf16[8,384,96]{1,2,0:T(8,128)(2,1)} all-gather(bf16[1,384,96]{1,2,0:T(8,128)(2,1)S(1)} %convert_element_type.142), channel_id=1, replica_groups=mesh['group'=8,'dp'=16] {'group'}, dimensions={0}, use_global_device_ids=true | all-gather | bytes 663552 | tf_op jit(solution)/shard_map/all_gather | solution.py:231
  54.5 18.8 %all-gather = bf16[8,3,24]{2,1,0:T(4,128)(2,1)S(1)} all-gather(bf16[1,3,24]{2,1,0:T(4,128)(2,1)S(1)} %convert_bitcast_fusion), channel_id=1, replica_groups=mesh['group'=8,'dp'=16] {'group'}, dimensions={0}, use_global_device_ids=true | all-gather | bytes 1296 | tf_op jit(solution)/shard_map/all_gather | solution.py:232
  73.4 30.3 %all_gather.16 = bf16[24,384]{0,1:T(8,128)(2,1)S(1)} all-gather(bf16[24,24]{0,1:T(8,128)(2,1)S(1)} %copy.130), channel_id=1, replica_groups=mesh['group'=8,'dp'=16] {'dp'}, dimensions={1}, use_global_device_ids=true | all-gather | bytes 19584 | tf_op jit(solution)/shard_map/all_gather | solution.py:236
  115.1 4.3 dynamic-slice_bitcast_fusion
  131.4 11.4 %fusion.16 = (bf16[577,1536]{1,0:T(8,128)(2,1)S(1)}, f32[577,1536]{1,0:T(8,128)}) fusion(f32[1536]{0:T(1024)S(1)} %add.326, bf16[8,384,1536]{1,2,0:T(8,128)(2,1)} %all-gather.4.cloned.1.call-done, s32[]{:T(128)S(6)} %select_n.66, f32[577,384]{1,0:T(8,128)S(1)} %get-tuple-element.121, f32[384]{0:T(512)S(1)} %get-tuple-element.73, ...), kind=kOutput, calls=%fused_computation.34 | convolution fusion | flops 740258688 | bytes 7397388 | tf_op jit(solution)/shard_map/dot_general | solution.py:103
  159.1 11.2 %fusion.19 = (bf16[577,1536]{1,0:T(8,128)(2,1)}, f32[577,1536]{1,0:T(8,128)S(1)}) fusion(f32[1536]{0:T(1024)S(1)} %add.351, bf16[8,384,1536]{1,2,0:T(8,128)(2,1)} %all-gather.4.cloned.1.call-done, s32[]{:T(128)S(6)} %select_n.70, f32[577,384]{1,0:T(8,128)S(1)} %get-tuple-element.129, f32[384]{0:T(512)S(1)} %get-tuple-element.65, ...), kind=kOutput, calls=%fused_computation.37 | convolution fusion | flops 740258688 | bytes 7397388 | tf_op jit(solution)/shard_map/dot_general | solution.py:103
  170.3 4.4 convert_reduce_fusion
  174.8 3.8 multiply_reduce_fusion.4
  182.3 6.2 fusion.79
  188.5 7.2 multiply_reduce_fusion.1
  195.7 10.2 multiply_convert_fusion.1
  205.9 3.8 fusion.86
  215.4 4.4 convert_reduce_fusion.1
  225.7 6.0 fusion.82
  231.8 6.9 multiply_reduce_fusion
  238.7 10.2 multiply_convert_fusion
  248.9 3.8 fusion.88
  275.3 15.6 %gather_fusion = f32[8,384,1536]{2,1,0:T(8,128)} fusion(f32[8,384,1536]{2,1,0:T(8,128)} %fusion.48, s32[1024]{0:T(1024)} %pad_clamp_fusion), kind=kCustom, calls=%fused_computation | custom fusion | bytes 37748768 | tf_op jit(solution)/shard_map/jit(_take)/gather | solution.py:280
  291.0 18.7 %copy.150 = f32[8,384,1536]{1,2,0:T(8,128)} copy(f32[8,384,1536]{2,1,0:T(8,128)} %gather_fusion) | data formatting | bytes 37748736 | tf_op jit(solution)/shard_map/jit(_take)/gather | solution.py:280
  309.6 12.9 %broadcast_select_fusion = f32[8,1,384,16,96]{2,4,3,0,1:T(8,128)} fusion(f32[8,1,384,16,96]{2,4,3,0,1:T(8,128)} %bitcast.244, pred[8]{0:T(512)(128)(4,1)S(1)} %copy-done.74), kind=kLoop, calls=%fused_computation.1 | loop fusion | flops 4718592 | bytes 37748744 | tf_op jit(solution)/shard_map/jit(_take)/select_n | solution.py:280
  325.6 654.1 %reduce-scatter.2.cloned.1.call-done = f32[1,384,96]{1,2,0:T(8,128)} async-done(((f32[128,384,96]{1,2,0:T(8,128)}), f32[1,384,96]{1,2,0:T(8,128)}) %reduce-scatter.2.cloned.1.call-update) | async-done | bytes 147472 | tf_op jit(solution)/shard_map/reduce_scatter | solution.py:287
  992.5 70.3 %all-reduce.4 = f32[384,24]{1,0:T(8,128)S(1)} all-reduce(f32[384,24]{1,0:T(8,128)S(1)} %reshape.357), channel_id=3, replica_groups=mesh['group'=8,'dp'=16] {'group','dp'}, use_global_device_ids=true, to_apply=%region_42.43.clone | all-reduce | flops 9216 | bytes 73728
  1067.3 4.1 fusion.70
  1072.6 4.0 fusion.52
  1076.7 4.2 fusion.67
  1082.2 4.0 fusion.53
  1086.2 4.0 fusion.64
  1091.5 4.2 fusion.54
  1095.7 4.0 fusion.61
  1101.0 4.0 fusion.55
  1105.0 4.3 fusion.58
  1110.6 3.9 convolution_bitcast_fusion
  (294 shorter events, 100.2 us)
Async XLA Ops:
  7.2 104.2 %copy-start.52 = (s32[8]{0:T(128)S(1)}, s32[8]{0:T(128)}, u32[]{:S(2)}) copy-start(s32[8]{0:T(128)} %param.13) | copy-start | bytes 100
  7.2 100.2 %copy-start.4 = (f32[1,577,384]{2,0,1:T(1,128)S(1)}, f32[1,577,384]{2,0,1:T(1,128)}, u32[]{:S(2)}) copy-start(f32[1,577,384]{2,0,1:T(1,128)} %param.10) | copy-start | bytes 2658820
  7.2 107.9 %all-gather.4.cloned.1.call-start = ((), (), s32[]{:S(2)}) async-start(), calls=%async_computation.1 | async-start | bytes 10027008 | tf_op jit(solution)/shard_map/all_gather | solution.py:235
  41.9 937.8 %reduce-scatter.2.cloned.1.call-start = ((), (), s32[]{:S(2)}) async-start(), calls=%async_computation.2 | async-start | bytes 19021824 | tf_op jit(solution)/shard_map/reduce_scatter | solution.py:287
  114.2 5.2 copy-start.58
  114.2 5.2 copy-start.64
  114.3 5.2 copy-start.54
  115.1 4.3 copy-start.56
  129.3 13.5 %copy-start.36 = (bf16[6,64,577]{2,1,0:T(8,128)(2,1)}, bf16[6,64,577]{2,1,0:T(8,128)(2,1)S(1)}, u32[]{:S(2)}) copy-start(bf16[6,64,577]{2,1,0:T(8,128)(2,1)S(1)} %fusion.78) | copy-start | bytes 1329412
  131.1 92.5 %copy-start.10 = (f32[577,384]{1,0:T(8,128)}, f32[577,384]{1,0:T(8,128)S(1)}, u32[]{:S(2)}) copy-start(f32[577,384]{1,0:T(8,128)S(1)} %get-tuple-element.121) | copy-start | bytes 2658820
  146.0 67.0 %copy-start.12 = (f32[577,384]{1,0:T(8,128)}, f32[577,384]{1,0:T(8,128)S(1)}, u32[]{:S(2)}) copy-start(f32[577,384]{1,0:T(8,128)S(1)} %get-tuple-element.125) | copy-start | bytes 2658820
  158.1 12.2 %copy-start.38 = (bf16[6,64,577]{2,1,0:T(8,128)(2,1)}, bf16[6,64,577]{2,1,0:T(8,128)(2,1)S(1)}, u32[]{:S(2)}) copy-start(bf16[6,64,577]{2,1,0:T(8,128)(2,1)S(1)} %fusion.77) | copy-start | bytes 1329412
  158.8 19.8 %copy-start.8 = (f32[577,384]{1,0:T(8,128)}, f32[577,384]{1,0:T(8,128)S(1)}, u32[]{:S(2)}) copy-start(f32[577,384]{1,0:T(8,128)S(1)} %get-tuple-element.129) | copy-start | bytes 2658820
  159.1 11.3 %copy-start.14 = (f32[1,577,384]{2,0,1:T(1,128)S(1)}, f32[1,577,384]{2,0,1:T(1,128)}, u32[]{:S(2)}) copy-start(f32[1,577,384]{2,0,1:T(1,128)} %param.11) | copy-start | bytes 2658820
  182.3 6.2 copy-start.22
  182.3 6.2 copy-start.27
  213.5 10.1 copy-start.6
  225.7 6.0 copy-start.25
  238.7 10.2 copy-start.17
  291.0 18.7 %copy-start.74 = (pred[8]{0:T(512)(128)(4,1)S(1)}, pred[8]{0:T(512)(128)(4,1)}, u32[]{:S(2)}) copy-start(pred[8]{0:T(512)(128)(4,1)} %compare_and_fusion) | copy-start | bytes 28
  322.5 658.9 %copy-start.63 = (f32[384]{0:T(512)S(1)}, f32[384]{0:T(512)}, u32[]{:S(2)}) copy-start(f32[384]{0:T(512)} %get-tuple-element.64) | copy-start | bytes 4612
  322.6 740.8 %all-gather.6.cloned.1.call-start = ((), (), s32[]{:S(2)}) async-start(), calls=%async_computation.3 | async-start | bytes 1253376 | tf_op jit(solution)/shard_map/all_gather | solution.py:298
  981.4 4.9 copy-start.33
  981.4 4.9 copy-start.35
  981.4 4.9 copy-start.43
  981.5 4.9 copy-start.48
  987.6 4.3 copy-start.67
  987.6 4.3 copy-start.66
  987.6 4.4 copy-start.60
  988.1 74.6 %copy-start.62 = (f32[3,24]{1,0:T(4,128)S(1)}, f32[3,24]{1,0:T(4,128)}, u32[]{:S(2)}) copy-start(f32[3,24]{1,0:T(4,128)} %param.16) | copy-start | bytes 868
  988.1 74.6 %copy-start.72 = (f32[3,24]{1,0:T(4,128)S(1)}, f32[3,24]{1,0:T(4,128)}, u32[]{:S(2)}) copy-start(f32[3,24]{1,0:T(4,128)} %param.18) | copy-start | bytes 868
  988.1 74.6 %copy-start.73 = (f32[3,24]{1,0:T(4,128)S(1)}, f32[3,24]{1,0:T(4,128)}, u32[]{:S(2)}) copy-start(f32[3,24]{1,0:T(4,128)} %param.17) | copy-start | bytes 868
  (51 other events, 130.0 us)
Sparse Core Ops, SparseCore 0:
  42.0 65.1 all-gather.3
  322.7 656.9 reduce-scatter.1
  982.0 33.7 all-gather.5
where the time goes:
time: 1130 us; the launch traced here: 1120 us
  waiting for transfers between devices  654 us (58%)
  matrix products  160 us (14%)
  blocking collectives  153 us (14%)
  local copies, waits for them, and re-layouts  71.2 us (6%)
  other arithmetic  50.4 us (4%)
  between operations  33.2 us (3%)
    reduce_scatter x1, waiting for transfers between devices, on_device(): lax.psum_scatter(spread_mats.reshape(-1, features, columns), ('group', 'd...  654 us
    unnamed x1, blocking collectives  70.3 us
    gather x2, local copies, waits for them, and re-layouts, on_device(): by_slot = jnp.take(stacked, mat_of, axis=0)  34.3 us
    all_gather x1, blocking collectives, on_device(): lax.all_gather(weights.astype(jnp.bfloat16), 'group', axis=0, tiled=True)  33.6 us
    all_gather x1, blocking collectives, on_device(): lax.all_gather(owner_vec, 'dp', axis=1, tiled=True)  30.3 us
    dot_general x2, matrix products, layer_forward(): jnp.dot(hidden_low, w_up, preferred_element_type=jnp.float32)  22.7 us
  transfers between devices with their start and end apart: 3, of which 1 were waited for; matrix products, arithmetic and copies ran while one was open for 2% of the time, Pallas kernels for 0%

commit v1 on v0

v1 whole, which is shorter than its diff:
```python
import jax
import jax.numpy as jnp
from jax import lax
from jax.experimental import pallas as pl
from jax.experimental.pallas import tpu as pltpu
from jax.sharding import PartitionSpec as P

HEADS = 6
FF = 1536
LAYERS = 2
NEWTON_STEPS = 5
STEP = 10
MATS = 8
VROWS = 24


norm_eps = 1e-06
ortho_eps = 1e-07
coef_a = 3.4445
coef_b = -4.775
coef_c = 2.0315
momentum_keep = 0.95
muon_rate = 0.25
muon_decay = 0.01
muon_shape = 0.5
adam_rate = 0.4
first_keep = 0.9
second_keep = 0.999
adam_eps = 1e-08
half_root = 0.7071067811865476
density = 0.3989422804014327


def normalize(values):
    center = values - jnp.mean(values, -1, keepdims=True)
    inv_std = lax.rsqrt(jnp.mean(center * center, -1, keepdims=True) + norm_eps)
    return (center * inv_std, inv_std)


def norm_back(upstream, normed, inv_std, gain):
    scaled = upstream * gain
    return inv_std * (
        scaled
        - jnp.mean(scaled, -1, keepdims=True)
        - normed * jnp.mean(scaled * normed, -1, keepdims=True)
    )


def gelu_slope(values):
    return (
        0.5 * (1.0 + lax.erf(values * half_root))
        + values * jnp.exp(-0.5 * values * values) * density
    )


def row_contract(left_op, right_op):
    return lax.dot_general(
        left_op, right_op, (((0,), (0,)), ((), ())), preferred_element_type=jnp.float32
    )


def col_contract(left_op, right_op):
    return lax.dot_general(
        left_op, right_op, (((1,), (1,)), ((), ())), preferred_element_type=jnp.float32
    )


BLK = 96
WIDE = 384
VPAD = 32
RINGX = 4
RINGZ = 4
STEPS = [(flip, hops) for flip in range(2) for hops in range(RINGZ)]


def half(part):
    return part.astype(jnp.bfloat16)


def full(part):
    return part.astype(jnp.float32)


def near(part, change):
    return lax.ppermute(part, "dp", [(at, change(at)) for at in range(16)])


def other_core(part):
    return near(part, lambda at: at ^ 1)


def other_row(part):
    return near(part, lambda at: at ^ 2)


def along_x(part, hops):
    return near(part, lambda at: (at + 4 * hops) % 16)


def along_group(part, flip, hops):
    pairs = [(at, (at ^ (4 * flip)) // 4 * 4 + (at + hops) % RINGZ) for at in range(8)]
    return lax.ppermute(part, "group", pairs)


def my_place():
    spot = lax.axis_index("dp")
    return spot >> 2, (spot >> 1) & 1, spot & 1


def my_group():
    group = lax.axis_index("group")
    return group >> 2, group & 3


def rows_at(start, count=BLK):
    return pl.ds(pl.multiple_of(start, 32), count)


def small_call(kernel, outs, ins, slot_first=False, scratch=(), name=None, vmem=32):
    specs = [pl.BlockSpec(memory_space=pltpu.VMEM)] * len(ins)
    if slot_first:
        specs[0] = pl.BlockSpec(memory_space=pltpu.SMEM)
    return pl.pallas_call(
        kernel,
        out_shape=[jax.ShapeDtypeStruct((rows, WIDE), kind) for rows, kind in outs],
        in_specs=specs,
        out_specs=[pl.BlockSpec(memory_space=pltpu.VMEM)] * len(outs),
        scratch_shapes=list(scratch),
        compiler_params=pltpu.CompilerParams(vmem_limit_bytes=vmem << 20),
        name=name,
    )(*ins)


def choose_kernel(slot_ref, *refs):
    blocks, (first_ref, second_ref, third_ref), hold = refs[:8], refs[8:11], refs[11]
    flip, z = my_group()
    spread = None
    for at, block in enumerate(blocks):
        hold[at] = block[:BLK]
        piece = full(block[BLK:])
        spread = piece if spread is None else spread + piece

    def matrix(mat_index):
        slot = slot_ref[mat_index]
        return hold[((slot >> 2) ^ flip) * RINGZ + ((slot - z) & 3)]

    first_ref[:BLK] = matrix(0)
    first_ref[BLK : 2 * BLK] = matrix(1)
    first_ref[2 * BLK :] = half(spread)
    second_ref[:BLK] = matrix(2)
    second_ref[BLK:] = matrix(3)
    for member in range(4):
        third_ref[member * BLK : (member + 1) * BLK] = matrix(4 + member)


def merge_x_kernel(heads, hidden, spread, *refs):
    parts, out_ref, hold = refs[:4], refs[4], refs[5]
    x, _, _ = my_place()
    for at in range(4):
        hold[at] = parts[at][...]
    put = 0
    if heads:
        for at in range(3):
            out_ref[at * BLK : (at + 1) * BLK] = hold[(at - x) & 3, :BLK]
        out_ref[3 * BLK : 4 * BLK] = hold[(0 - x) & 3, BLK : 2 * BLK]
        put = 4 * BLK
    if hidden:
        base = 2 * BLK if heads else 0
        for member in range(2):
            for at in range(4):
                start = base + member * BLK
                out_ref[put : put + BLK] = parts[at][start : start + BLK]
                put += BLK
    if spread:
        base = parts[0].shape[0] - VPAD
        total = full(parts[0][base:])
        for at in range(1, 4):
            total = total + full(parts[at][base:])
        out_ref[put : put + VPAD] = half(total)


def final_kernel(heads, hidden, spread, *refs):
    parts, outs = refs[:4], list(refs[4:])
    _, row, core = my_place()
    base = 0
    if heads:
        qkv_ref, out_ref = outs[:2]
        outs = outs[2:]
        for at_part, part in enumerate(parts):
            piece = (row ^ (at_part & 1)) * 2 * BLK + (core ^ (at_part >> 1)) * BLK
            for at in range(3):
                qkv_ref[rows_at(at * WIDE + piece)] = part[at * BLK : (at + 1) * BLK]
            out_ref[rows_at(piece)] = part[3 * BLK : 4 * BLK]
        base = 4 * BLK
    if hidden:
        for member in range(2):
            for at_part, part in enumerate(parts):
                start = base + member * WIDE
                outs[member][at_part * WIDE : (at_part + 1) * WIDE] = part[start : start + WIDE]
        base += 2 * WIDE
        outs = outs[2:]
    if spread:
        total = full(parts[0][base:])
        for part in parts[1:]:
            total = total + full(part[base:])
        outs[0][...] = total


def gather_steps(part, heads, hidden, spread, name):
    rows = 4 * BLK * heads + 8 * BLK * hidden + VPAD * spread
    parts = [part] + [along_x(part, -hops) for hops in (1, 2, 3)]
    (own,) = small_call(
        lambda *refs: merge_x_kernel(heads, hidden, spread, *refs),
        [(rows, jnp.bfloat16)],
        parts,
        scratch=[pltpu.VMEM((4, *part.shape), jnp.bfloat16)],
        name=name + "_merge_x",
    )
    return own, rows


def gather_last(own, heads, hidden, spread, name):
    beside = other_row(own)
    parts = [own, beside, other_core(own), other_core(beside)]
    outs = []
    if heads:
        outs += [(3 * WIDE, jnp.bfloat16), (WIDE, jnp.bfloat16)]
    if hidden:
        outs += [(FF, jnp.bfloat16)] * 2
    if spread:
        outs += [(VPAD, jnp.float32)]
    return small_call(
        lambda *refs: final_kernel(heads, hidden, spread, *refs), outs, parts, name=name + "_whole"
    )


def put_vec(ref, start, value):
    high = half(value)
    ref[start : start + VPAD] = high
    ref[start + VPAD : start + 2 * VPAD] = half(value - full(high))


def get_vec(ref, start):
    return full(ref[start : start + VPAD]) + full(ref[start + VPAD : start + 2 * VPAD])


def split_core_kernel(heads, hidden, spread, *refs):
    refs = list(refs)
    keep_ref, sent_ref = refs[-2:]
    _, _, core = my_place()
    put = 0
    if heads:
        qkv_ref, out_ref = refs[:2]
        refs = refs[2:]
        for row in range(2):
            for at in range(4):
                source = out_ref if at == 3 else qkv_ref
                start = (0 if at == 3 else at * WIDE) + row * 2 * BLK
                keep_ref[put : put + BLK] = source[rows_at(start + core * BLK)]
                sent_ref[put : put + BLK] = source[rows_at(start + (1 - core) * BLK)]
                put += BLK
    if hidden:
        for source in refs[:2]:
            keep_ref[put : put + 2 * WIDE] = source[: 2 * WIDE]
            sent_ref[put : put + 2 * WIDE] = source[2 * WIDE :]
            put += 2 * WIDE
        refs = refs[2:]
    if spread:
        put_vec(sent_ref, put, refs[0][...])


def split_row_kernel(heads, hidden, spread, *refs):
    had_ref, came_ref = refs[:2]
    keep_ref, sent_ref = refs[2 + spread : 4 + spread]
    _, row, _ = my_place()

    def total(start):
        at = rows_at(start, WIDE)
        return full(had_ref[at]) + full(came_ref[at])

    put, base = 0, 0
    if heads:
        keep_ref[:WIDE] = total(row * WIDE)
        sent_ref[:WIDE] = half(total((1 - row) * WIDE))
        put, base = WIDE, 2 * WIDE
    if hidden:
        for _ in range(2):
            keep_ref[put : put + WIDE] = total(base)
            sent_ref[put : put + WIDE] = half(total(base + WIDE))
            put, base = put + WIDE, base + 2 * WIDE
    if spread:
        value = refs[2][...] + get_vec(came_ref, base)
        refs[-1][...] = value
        put_vec(sent_ref, put, value)


def split_x_kernel(heads, hidden, spread, *refs):
    had_ref, came_ref = refs[:2]
    keep_ref, *sent_refs = refs[2 + spread : 6 + spread]
    hold = refs[-1]
    x, _, _ = my_place()
    count = had_ref.shape[0]
    hold[...] = had_ref[...] + full(came_ref[:count])
    for hops, target in enumerate([keep_ref] + sent_refs):
        kind = target.dtype
        put, base = 0, 0
        if heads:
            at = (x + hops) & 3
            piece = hold[rows_at(at * BLK)]
            target[:BLK] = jnp.where(at == 3, 0.0, piece).astype(kind)
            target[BLK : 2 * BLK] = hold[3 * BLK : 4 * BLK].astype(kind)
            put, base = 2 * BLK, WIDE
        if hidden:
            for _ in range(2):
                start = base + hops * BLK
                target[put : put + BLK] = hold[start : start + BLK].astype(kind)
                put, base = put + BLK, base + WIDE
        if spread and hops:
            value = refs[2][...] + get_vec(came_ref, base)
            refs[-2][...] = value
            put_vec(target, put, value)


def sum_x_kernel(heads, keep_ref, *refs):
    parts, out_ref = refs[:3], refs[3]
    x, _, _ = my_place()
    total = keep_ref[...]
    for part in parts:
        total = total + full(part[...])
    out_ref[...] = total
    if heads:
        out_ref[BLK : 2 * BLK] = jnp.where(x == 0, total[BLK : 2 * BLK], 0.0)


def scatter_core(grads, heads, hidden, spread, name):
    rows = 8 * BLK * heads + 16 * BLK * hidden
    keep, sent = small_call(
        lambda *refs: split_core_kernel(heads, hidden, spread, *refs),
        [(rows, jnp.bfloat16), (rows + 2 * VPAD * spread, jnp.bfloat16)],
        grads,
        name=name + "_split_core",
    )
    return keep, sent


def scatter_row(keep, came, heads, hidden, spread, name, vec_sum=None):
    rows = 4 * BLK * heads + 8 * BLK * hidden
    return small_call(
        lambda *refs: split_row_kernel(heads, hidden, spread, *refs),
        [(rows, jnp.float32), (rows + 2 * VPAD * spread, jnp.bfloat16)]
        + [(VPAD, jnp.float32)] * spread,
        [keep, came] + [vec_sum] * spread,
        name=name + "_split_row",
    )


def scatter_x(keep, came, heads, hidden, spread, name, vec_sum=None):
    rows = 2 * BLK * heads + 2 * BLK * hidden
    return small_call(
        lambda *refs: split_x_kernel(heads, hidden, spread, *refs),
        [(rows, jnp.float32)]
        + [(rows + 2 * VPAD * spread, jnp.bfloat16)] * 3
        + [(VPAD, jnp.float32)] * spread,
        [keep, came] + [vec_sum] * spread,
        scratch=[pltpu.VMEM(keep.shape, jnp.float32)],
        name=name + "_split_x",
    )


def spread_x(sent):
    return [along_x(part, hops + 1) for hops, part in enumerate(sent)]


def split_group_kernel(slot_ref, *refs):
    second_ref, third_ref, keep_ref, *parts = refs[:6]
    vec_ref, own_ref = refs[6], refs[7]
    sent_refs, vec_out, hold = refs[8:15], refs[15], refs[16]
    flip, z = my_group()
    x, _, _ = my_place()
    total = keep_ref[...]
    value = vec_ref[...]
    for part in parts:
        total = total + full(part[: 2 * BLK])
        value = value + get_vec(part, 2 * BLK)
    vec_out[...] = value
    hold[0] = total[:BLK]
    hold[1] = jnp.where(x == 0, total[BLK:], 0.0)
    for member in range(2):
        hold[2 + member] = second_ref[member * BLK : (member + 1) * BLK]
    for member in range(4):
        hold[4 + member] = third_ref[member * BLK : (member + 1) * BLK]
    for at, (turn, hops) in enumerate(STEPS):
        slot = (flip ^ turn) * RINGZ + ((z + hops) & 3)
        mat_index = jnp.int32(0)
        for member in range(1, MATS):
            mat_index = jnp.where(slot_ref[member] == slot, member, mat_index)
        if at == 0:
            own_ref[...] = hold[mat_index]
        else:
            sent_refs[at - 1][:BLK] = half(hold[mat_index])
            put_vec(sent_refs[at - 1], BLK, value)


def renew_kernel(own_ref, *refs):
    parts, (vec_ref, moment_ref) = refs[:7], refs[7:9]
    grad_ref, new_ref, low_ref, vec_out = refs[9:]
    total, value = own_ref[...], vec_ref[...]
    for part in parts:
        total = total + full(part[:BLK])
        value = value + get_vec(part, BLK)
    grad_ref[...] = total
    vec_out[...] = value
    renewed = momentum_keep * moment_ref[...] + total
    new_ref[...] = renewed
    low_ref[...] = half(renewed)


def split_dot(left, right):
    left_high, right_high = half(left), half(right)
    left_low, right_low = half(left - full(left_high)), half(right - full(right_high))

    def product(one, two):
        return jnp.dot(one, two, preferred_element_type=jnp.float32)

    return product(left_high, right_high) + (
        product(left_high, right_low) + product(left_low, right_high)
    )


def newton_kernel(slot_ref, *refs):
    parts, own_ref, weight_ref, out_ref = refs[:4], refs[4], refs[5], refs[6]
    size = WIDE
    gram = None
    for part in parts:
        piece = row_contract(part[...], part[...])
        gram = piece if gram is None else gram + piece
    diagonal = lax.broadcasted_iota(jnp.int32, (size, size), 0) == lax.broadcasted_iota(
        jnp.int32, (size, size), 1
    )
    trace = jnp.sum(jnp.where(diagonal, gram, 0.0), keepdims=True)
    inverse = 1.0 / (jnp.sqrt(trace) + ortho_eps)
    gram = gram * inverse * inverse
    total = None
    for iteration in range(NEWTON_STEPS):
        squared = split_dot(gram, gram)
        step = jnp.where(diagonal, coef_a, 0.0) + coef_b * gram + coef_c * squared
        total = step if total is None else split_dot(step, total)
        if iteration < NEWTON_STEPS - 1:
            gram = split_dot(step, split_dot(step, gram))
    total = total * inverse
    high = half(total)
    low = half(total - full(high))
    own = own_ref[...]
    ortho = jnp.dot(own, high, preferred_element_type=jnp.float32) + jnp.dot(
        own, low, preferred_element_type=jnp.float32
    )
    group = lax.axis_index("group")
    widths = [3 * WIDE, WIDE, FF, FF] * LAYERS
    scale = jnp.float32(0.0)
    for member in range(MATS):
        rate = muon_rate * muon_shape * widths[member] ** 0.5
        scale = jnp.where(slot_ref[member] == group, jnp.float32(rate), scale)
    out_ref[...] = weight_ref[...] * (1.0 - muon_rate * muon_decay) - scale * ortho


def turned(part):
    return half(full(part).T)


def attend_kernel(q_ref, k_ref, v_ref, out_ref, prob_ref):
    queries, keys, values = q_ref[...], k_ref[...], v_ref[...]
    queries = queries * jnp.bfloat16(0.125)
    lane = lax.broadcasted_iota(jnp.int32, keys.shape, 1)
    values_t = turned(values)
    sums = []
    for head in range(2):
        mine = half(jnp.where((lane >> 6) == head, 1.0, 0.0))
        scores = col_contract(keys * mine, queries)
        exponent = jnp.exp(scores - jnp.max(scores, 0, keepdims=True))
        probs = half(exponent * (1.0 / jnp.sum(exponent, 0, keepdims=True)))
        prob_ref[head] = probs
        sums.append(jnp.dot(values_t, probs, preferred_element_type=jnp.float32))
    row = lax.broadcasted_iota(jnp.int32, sums[0].shape, 0)
    out_ref[...] = half(jnp.where(row < 64, sums[0], sums[1]).T)


def attend(qkv_low):
    length = qkv_low.shape[0]

    def part(offset):
        return pl.BlockSpec((length, 128), lambda at: (0, offset + at))

    return pl.pallas_call(
        attend_kernel,
        grid=(HEADS // 2,),
        out_shape=[
            jax.ShapeDtypeStruct((length, WIDE), jnp.bfloat16),
            jax.ShapeDtypeStruct((HEADS, length, length), jnp.bfloat16),
        ],
        in_specs=[part(0), part(3), part(6)],
        out_specs=[part(0), pl.BlockSpec((2, length, length), lambda at: (at, 0, 0))],
        compiler_params=pltpu.CompilerParams(vmem_limit_bytes=32 << 20),
        cost_estimate=pl.CostEstimate(
            flops=4 * HEADS * length * length * 64 * 4,
            bytes_accessed=HEADS * length * length * 2 + 4 * length * WIDE * 2,
            transcendentals=HEADS * length * length,
        ),
        name="attend",
    )(qkv_low, qkv_low, qkv_low)


def attend_back_kernel(q_ref, k_ref, v_ref, up_ref, prob_ref, out_ref):
    queries, keys, values, upstream = q_ref[...], k_ref[...], v_ref[...], up_ref[...]
    lane = lax.broadcasted_iota(jnp.int32, keys.shape, 1)
    keys_t = turned(keys)
    got = []
    for head in range(2):
        mine = half(jnp.where((lane >> 6) == head, 1.0, 0.0))
        probs_low = prob_ref[head]
        probs = full(probs_low)
        prob_grad = col_contract(values * mine, upstream)
        inner = jnp.sum(prob_grad * probs, 0, keepdims=True)
        score_low = half(probs * (prob_grad - inner))
        got.append(
            (
                jnp.dot(keys_t, score_low, preferred_element_type=jnp.float32),
                jnp.dot(score_low, queries, preferred_element_type=jnp.float32),
                jnp.dot(probs_low, upstream, preferred_element_type=jnp.float32),
            )
        )
    row = lax.broadcasted_iota(jnp.int32, got[0][0].shape, 0)
    at = pl.program_id(0)
    query_grad = jnp.where(row < 64, got[0][0], got[1][0]).T * 0.125
    key_grad = jnp.where(lane < 64, got[0][1], got[1][1]) * 0.125
    value_grad = jnp.where(lane < 64, got[0][2], got[1][2])
    for third, value in enumerate((query_grad, key_grad, value_grad)):
        out_ref[:, pl.ds(pl.multiple_of(third * WIDE + at * 128, 128), 128)] = half(value)


def attend_back(qkv_low, attn_grad, probs):
    length = qkv_low.shape[0]

    def part(offset):
        return pl.BlockSpec((length, 128), lambda at: (0, offset + at))

    return pl.pallas_call(
        attend_back_kernel,
        grid=(HEADS // 2,),
        out_shape=jax.ShapeDtypeStruct(qkv_low.shape, jnp.bfloat16),
        in_specs=[
            part(0),
            part(3),
            part(6),
            part(0),
            pl.BlockSpec((2, length, length), lambda at: (at, 0, 0)),
        ],
        out_specs=pl.BlockSpec(qkv_low.shape, lambda at: (0, 0)),
        compiler_params=pltpu.CompilerParams(vmem_limit_bytes=32 << 20),
        cost_estimate=pl.CostEstimate(
            flops=8 * HEADS * length * length * 64 * 4,
            bytes_accessed=HEADS * length * length * 2 + 8 * length * WIDE * 2,
            transcendentals=0,
        ),
        name="attend_back",
    )(qkv_low, qkv_low, qkv_low, attn_grad, probs)


def attention_forward(inputs, w_qkv, w_out, vec_rows):
    normed_one, inv_one = normalize(inputs)
    normed_low = half(normed_one * vec_rows[0] + vec_rows[1])
    qkv_bias = jnp.concatenate([vec_rows[2], jnp.zeros_like(vec_rows[2]), vec_rows[3]])
    qkv_low = half(col_contract(normed_low, w_qkv) + qkv_bias)
    attn_low, probs = attend(qkv_low)
    middle = inputs + (col_contract(attn_low, w_out) + vec_rows[4])
    return middle, (normed_one, inv_one, normed_low, qkv_low, probs, attn_low)


def hidden_forward(middle, w_up, w_down, vec_rows, bias_up):
    normed_two, inv_two = normalize(middle)
    hidden_low = half(normed_two * vec_rows[5] + vec_rows[6])
    hidden = col_contract(hidden_low, w_up) + bias_up
    active_low = half(jax.nn.gelu(hidden, approximate=False))
    result = middle + (jnp.dot(active_low, w_down, preferred_element_type=jnp.float32) + vec_rows[7])
    return result, (normed_two, inv_two, hidden_low, hidden, active_low)


def hidden_backward(upstream, w_up, w_down, vec_rows, stored):
    normed_two, inv_two, hidden_low, hidden, active_low = stored
    down_low = half(upstream)
    grad_down = half(row_contract(active_low, down_low))
    up_low = half(col_contract(down_low, w_down) * gelu_slope(hidden))
    grad_up = half(row_contract(up_low, hidden_low))
    back_hidden = jnp.dot(up_low, w_up, preferred_element_type=jnp.float32)
    middle_grad = upstream + norm_back(back_hidden, normed_two, inv_two, vec_rows[5])
    sums = [
        jnp.sum(back_hidden * normed_two, 0),
        jnp.sum(back_hidden, 0),
        jnp.sum(full(down_low), 0),
    ]
    return middle_grad, grad_up, grad_down, sums, jnp.sum(full(up_low), 0)


def attention_backward(middle_grad, w_qkv, w_out, vec_rows, stored):
    normed_one, inv_one, normed_low, qkv_low, probs, attn_low = stored
    out_low = half(middle_grad)
    grad_out = half(row_contract(out_low, attn_low))
    attn_grad = half(jnp.dot(out_low, w_out, preferred_element_type=jnp.float32))
    qkv_grad = attend_back(qkv_low, attn_grad, probs)
    grad_qkv = half(row_contract(qkv_grad, normed_low))
    back_normed = jnp.dot(qkv_grad, w_qkv, preferred_element_type=jnp.float32)
    input_grad = middle_grad + norm_back(back_normed, normed_one, inv_one, vec_rows[0])
    qkv_sum = jnp.sum(full(qkv_grad), 0)
    sums = [
        jnp.sum(back_normed * normed_one, 0),
        jnp.sum(back_normed, 0),
        qkv_sum[:WIDE],
        qkv_sum[2 * WIDE :],
        jnp.sum(full(out_low), 0),
    ]
    return input_grad, grad_qkv, grad_out, sums


def turn(parts, count):
    turned_parts = [jnp.roll(parts, -by, 0) for by in range(RINGX)]
    low = jnp.where((count & 1) == 0, turned_parts[0], turned_parts[1])
    high = jnp.where((count & 1) == 0, turned_parts[2], turned_parts[3])
    return jnp.where((count & 2) == 0, low, high)


def swap(parts, flag, axis):
    return jnp.where(flag == 0, parts, jnp.flip(parts, axis))


def to_own_order(row, place):
    cube = row.reshape(RINGX, 2, 2, BLK)
    cube = turn(swap(swap(cube, place[2], 2), place[1], 1), place[0])
    return cube.transpose(2, 1, 0, 3).reshape(-1)


def from_own_order(row, place):
    cube = row.reshape(2, 2, RINGX, BLK).transpose(2, 1, 0, 3)
    cube = swap(swap(turn(cube, (4 - place[0]) & 3), place[2], 2), place[1], 1)
    return cube.reshape(-1)


def on_device(tokens, cotangent, live, slot_of, weights, momentum, vec, vec_first, vec_second):
    place = my_place()
    group_at = lax.axis_index("group")
    data_at = lax.axis_index("dp")
    vec_here, vec_cols = vec.shape
    per_layer = VROWS // LAYERS
    tie = lax.optimization_barrier
    spread = lax.dynamic_update_slice(
        jnp.zeros((VPAD, WIDE), jnp.bfloat16),
        half(vec),
        (group_at * vec_here, data_at * vec_cols),
    )
    own_block = jnp.concatenate([half(weights[0].T), spread], 0)
    slots = [own_block] + [along_group(own_block, flip, -hops) for flip, hops in STEPS[1:]]
    first, second, third = small_call(
        choose_kernel,
        [(2 * BLK + VPAD, jnp.bfloat16), (2 * BLK, jnp.bfloat16), (4 * BLK, jnp.bfloat16)],
        [slot_of] + slots,
        slot_first=True,
        scratch=[pltpu.VMEM((MATS, BLK, WIDE), jnp.bfloat16)],
        name="choose",
    )
    first_x, _ = gather_steps(first, True, False, True, "first")
    second, first_x = tie((second, first_x))
    second_x, _ = gather_steps(second, False, True, False, "second")
    w_qkv0, w_out0, vec_full = gather_last(first_x, True, False, True, "first")
    third, second_x = tie((third, second_x))
    third_x, _ = gather_steps(third, True, True, False, "third")
    w_up0, w_down0 = gather_last(second_x, False, True, False, "second")
    w_qkv1, w_out1, w_up1, w_down1 = gather_last(third_x, True, True, False, "third")
    rows0, rows1 = vec_full[:per_layer], vec_full[per_layer:VROWS]
    bias0 = to_own_order(rows0[8:].reshape(-1), place)
    bias1 = to_own_order(rows1[8:].reshape(-1), place)

    middle, attn0 = attention_forward(tokens[0], w_qkv0, w_out0, rows0)
    stream, mlp0 = hidden_forward(middle, w_up0, w_down0, rows0, bias0)
    middle, attn1 = attention_forward(stream, w_qkv1, w_out1, rows1)
    stream, mlp1 = hidden_forward(middle, w_up1, w_down1, rows1, bias1)

    upstream = cotangent[0] * full(live)[0]
    mid_grad, grad_up, grad_down, sums_two1, sums_up1 = hidden_backward(
        upstream, w_up1, w_down1, rows1, mlp1
    )
    upstream, grad_qkv, grad_out, sums_one1 = attention_backward(
        mid_grad, w_qkv1, w_out1, rows1, attn1
    )
    keep, sent = scatter_core([grad_qkv, grad_out, grad_up, grad_down], True, True, False, "third")
    upstream, sent = tie((upstream, sent))
    came = other_core(sent)
    mid_grad, grad_up, grad_down, sums_two0, sums_up0 = hidden_backward(
        upstream, w_up0, w_down0, rows0, mlp0
    )
    keep, sent = scatter_row(keep, came, True, True, False, "third")
    keep_f, sent_f = scatter_core([grad_up, grad_down], False, True, False, "second")
    mid_grad, sent, sent_f = tie((mid_grad, sent, sent_f))
    came = other_row(sent)
    came_f = other_core(sent_f)
    token_grad, grad_qkv, grad_out, sums_one0 = attention_backward(
        mid_grad, w_qkv0, w_out0, rows0, attn0
    )
    keep_f, sent_f = scatter_row(keep_f, came_f, False, True, False, "second")
    keep, *sent_x = scatter_x(keep, came, True, True, False, "third")

    def by_layer(one, two, sums_up):
        return one[:4] + [one[4]] + two + [
            from_own_order(sums_up, place).reshape(-1, WIDE)
        ]

    def vec_rows_of(parts):
        return jnp.concatenate([part.reshape(-1, WIDE) for part in parts], 0)

    vec_sum = jnp.concatenate(
        [
            vec_rows_of(by_layer(sums_one0, sums_two0, sums_up0)),
            vec_rows_of(by_layer(sums_one1, sums_two1, sums_up1)),
            jnp.zeros((VPAD - VROWS, WIDE), jnp.float32),
        ],
        0,
    )
    keep_h, sent_h = scatter_core([grad_qkv, grad_out, vec_sum], True, False, True, "first")
    sent_h, sent_f = tie((sent_h, sent_f))
    came_h = other_core(sent_h)
    came_f = other_row(sent_f)
    came_x = spread_x(sent_x)
    keep_h, sent_h, vec_sum = scatter_row(keep_h, came_h, True, False, True, "first", vec_sum)
    came_h = other_row(sent_h)
    keep_f, *sent_f = scatter_x(keep_f, came_f, False, True, False, "second")
    (third_sum,) = small_call(
        lambda *refs: sum_x_kernel(True, *refs),
        [(4 * BLK, jnp.float32)],
        [keep] + came_x,
        name="third_sum_x",
    )
    came_f = spread_x(sent_f)
    (second_sum,) = small_call(
        lambda *refs: sum_x_kernel(False, *refs),
        [(2 * BLK, jnp.float32)],
        [keep_f] + came_f,
        name="second_sum_x",
    )
    keep_h, *sent_h, vec_sum = scatter_x(keep_h, came_h, True, False, True, "first", vec_sum)
    came_h = spread_x(sent_h)
    own, *sent_g, vec_sum = small_call(
        split_group_kernel,
        [(BLK, jnp.float32)]
        + [(BLK + 2 * VPAD, jnp.bfloat16)] * 7
        + [(VPAD, jnp.float32)],
        [slot_of, second_sum, third_sum, keep_h] + came_h + [vec_sum],
        slot_first=True,
        scratch=[pltpu.VMEM((MATS, BLK, WIDE), jnp.float32)],
        name="split_group",
    )
    came_g = [along_group(part, flip, hops) for part, (flip, hops) in zip(sent_g, STEPS[1:])]
    grad_rows, moment_rows, moment_low, vec_sum = small_call(
        renew_kernel,
        [(BLK, jnp.float32), (BLK, jnp.float32), (BLK, jnp.bfloat16), (VPAD, jnp.float32)],
        [own] + came_g + [vec_sum, momentum[0].T],
        name="renew",
    )
    ring = jnp.concatenate([moment_low] + [along_x(moment_low, -hops) for hops in (1, 2, 3)], 0)
    beside = other_row(ring)
    (weight_rows,) = small_call(
        newton_kernel,
        [(BLK, jnp.float32)],
        [slot_of, ring, beside, other_core(ring), other_core(beside), moment_low, weights[0].T],
        slot_first=True,
        name="newton",
    )
    shard_vec = lax.dynamic_slice(
        vec_sum, (group_at * vec_here, data_at * vec_cols), (vec_here, vec_cols)
    )
    first_new = first_keep * vec_first + (1.0 - first_keep) * shard_vec
    second_new = second_keep * vec_second + (1.0 - second_keep) * shard_vec * shard_vec
    vec_new = vec - adam_rate * (
        first_new
        / (1.0 - first_keep**STEP)
        / (jnp.sqrt(second_new / (1.0 - second_keep**STEP)) + adam_eps)
    )
    return (
        stream[None],
        token_grad[None],
        grad_rows.T[None],
        moment_rows.T[None],
        weight_rows.T[None],
        first_new,
        second_new,
        vec_new,
    )


def solution(mesh):
    placed = (
        P(("group", "dp"), None, None),
        P(("group", "dp"), None, None),
        P(("group", "dp")),
        P(),
        P("group", None, "dp"),
        P("group", None, "dp"),
        P("group", "dp"),
        P("group", "dp"),
        P("group", "dp"),
    )
    return jax.shard_map(
        on_device,
        mesh=mesh,
        in_specs=placed,
        out_specs=(
            P(("group", "dp"), None, None),
            P(("group", "dp"), None, None),
            P("group", None, "dp"),
            P("group", None, "dp"),
            P("group", None, "dp"),
            P("group", "dp"),
            P("group", "dp"),
            P("group", "dp"),
        ),
        check_vma=False,
    )
```

time: 1130 us -> 303 us (0.27)
  waiting for transfers between devices: 654 us -> 66 us
  blocking collectives: 153 us -> 0 us
  matrix products: 160 us -> 49.4 us
  starting transfers between devices: 0.12 us -> 97.7 us
  Pallas kernels: 0 us -> 56 us
  local copies, waits for them, and re-layouts: 71.2 us -> 16.4 us
  other arithmetic: 50.4 us -> 12.5 us
  between operations: 33.2 us -> 2.66 us
    reduce_scatter x1 -> x0, waiting for transfers between devices: 654 us -> none  [on_device(): lax.psum_scatter(spread_mats.reshape(-1, features, columns), ('group', 'd...]
    dot_general x35 -> x8, matrix products: 127 us -> 10.6 us  [the longest x2 5.08 us: hidden_backward(): back_hidden = jnp.dot(up_low, w_up, preferred_element_type=jnp.float32)]
    ppermute x0 -> x53, starting transfers between devices: none -> 97.7 us  [the longest x39 69.4 us: near(): return lax.ppermute(part, 'dp', [(at, change(at)) for at in range(16)])]
    all_gather x3 -> x0, blocking collectives: 82.7 us -> none  [the longest x1 33.6 us: on_device(): lax.all_gather(weights.astype(jnp.bfloat16), 'group', axis=0, tiled=True)]
    unnamed x1 -> x0, blocking collectives: 70.3 us -> none
    ppermute x0 -> x53, waiting for transfers between devices: none -> 66 us  [the longest x39 54.5 us: near(): return lax.ppermute(part, 'dp', [(at, change(at)) for at in range(16)])]
    pallas_call x0 -> x25, Pallas kernels: none -> 56 us  [the longest x21 28.5 us: small_call(): pl.pallas_call(kernel, out_shape=[jax.ShapeDtypeStruct((rows, WIDE), kind...]
    gather x2 -> x0, local copies, waits for them, and re-layouts: 34.3 us -> none  [on_device(): by_slot = jnp.take(stacked, mat_of, axis=0)]
  transfers between devices with their start and end apart: 3 -> 53, of which waited for: 1 -> 19; matrix products, arithmetic and copies ran while one was open for 2% -> 13% of each run, Pallas kernels for 0% -> 5%
where the time goes in v1:
time: 303 us; the launch traced here: 301 us
  starting transfers between devices  97.7 us (32%)
  waiting for transfers between devices  66 us (22%)
  Pallas kernels  56 us (18%)
  matrix products  49.4 us (16%)
  local copies, waits for them, and re-layouts  16.4 us (5%)
  other arithmetic  12.5 us (4%)
    ppermute x39, starting transfers between devices, near(): return lax.ppermute(part, 'dp', [(at, change(at)) for at in range(16)])  69.4 us
    ppermute x39, waiting for transfers between devices, near(): return lax.ppermute(part, 'dp', [(at, change(at)) for at in range(16)])  54.5 us
    dot_general x8, matrix products, col_contract(): lax.dot_general(left_op, right_op, (((1,), (1,)), ((), ())), preferred_el...  28.6 us
    pallas_call x21, Pallas kernels, small_call(): pl.pallas_call(kernel, out_shape=[jax.ShapeDtypeStruct((rows, WIDE), kind...  28.5 us
    ppermute x14, starting transfers between devices, along_group(): return lax.ppermute(part, 'group', pairs)  28.3 us
    pallas_call x2, Pallas kernels, attend_back(): pl.pallas_call(attend_back_kernel, grid=(HEADS // 2,), out_shape=jax.Shap...  15.5 us
    unnamed x93, local copies, waits for them, and re-layouts  14.9 us
    pallas_call x2, Pallas kernels, attend(): pl.pallas_call(attend_kernel, grid=(HEADS // 2,), out_shape=[jax.ShapeDty...  12 us
  transfers between devices with their start and end apart: 53, of which 19 were waited for; matrix products, arithmetic and copies ran while one was open for 13% of the time, Pallas kernels for 5%

profile of v1, /device:TPU:1, one launch (start us, length us, event | category | flops | bytes accessed | tf_op | source)
XLA Modules:
  0.0 300.7 jit_solution(7287378850764713479)
XLA Ops:
  2.8 4.7 %collective-permute-start = (bf16[128,384]{1,0:T(8,128)(2,1)S(1)}, bf16[128,384]{1,0:T(8,128)(2,1)S(1)}, u32[]{:S(2)}, u32[]{:S(2)}) collective-permute-start(bf16[128,384]{1,0:T(8,128)(2,1)S(1)} %pad_maximum_fusion.refs_0_), channel_id=1, source_target_pairs={{0,48},{16,0},{32,16},{48,32},{64,112},{80,64},{96,80},{112,96},{1... | collective-permute-start | bytes 294920 | tf_op jit(solution)/shard_map/ppermute | solution.py:102
  8.2 2.9 collective-permute-start.3
  12.8 4.4 %collective-permute-start.5 = (bf16[128,384]{1,0:T(8,128)(2,1)S(1)}, bf16[128,384]{1,0:T(8,128)(2,1)S(1)}, u32[]{:S(2)}, u32[]{:S(2)}) collective-permute-start(bf16[128,384]{1,0:T(8,128)(2,1)S(1)} %pad_maximum_fusion.refs_0_), channel_id=1, source_target_pairs={{0,96},{16,112},{32,64},{48,80},{64,32},{80,48},{96,0},{112,16},{1... | collective-permute-start | bytes 294920 | tf_op jit(solution)/shard_map/ppermute | solution.py:102
  20.3 4.0 %collective-permute-done.6.refs_7_ = bf16[128,384]{1,0:T(8,128)(2,1)S(1)} collective-permute-done((bf16[128,384]{1,0:T(8,128)(2,1)S(1)}, bf16[128,384]{1,0:T(8,128)(2,1)S(1)}, u32[]{:S(2)}, u32[]{:S(2)}) %collective-permute-start.6) | collective-permute-done | bytes 98336 | tf_op jit(solution)/shard_map/ppermute | solution.py:102
  29.3 3.0 %collective-permute-done.7.refs_1_ = bf16[224,384]{1,0:T(8,128)(2,1)S(1)} collective-permute-done((bf16[224,384]{1,0:T(8,128)(2,1)S(1)}, bf16[224,384]{1,0:T(8,128)(2,1)S(1)}, u32[]{:S(2)}, u32[]{:S(2)}) %collective-permute-start.7) | collective-permute-done | bytes 172064 | tf_op jit(solution)/shard_map/ppermute | solution.py:85
  41.4 5.1 %collective-permute-start.11 = (bf16[416,384]{1,0:T(8,128)(2,1)S(1)}, bf16[416,384]{1,0:T(8,128)(2,1)S(1)}, u32[]{:S(2)}, u32[]{:S(2)}) collective-permute-start(bf16[416,384]{1,0:T(8,128)(2,1)S(1)} %first_merge_x.1.refs_0_), channel_id=1, source_target_pairs={{0,1},{1,0},{2,3},{3,2},{4,5},{5,4},{6,7},{7,6},{8,9},{9,8},{10,11... | collective-permute-start | bytes 958472 | tf_op jit(solution)/shard_map/ppermute | solution.py:85
  51.1 4.3 %collective-permute-start.12 = (bf16[416,384]{1,0:T(8,128)(2,1)S(1)}, bf16[416,384]{1,0:T(8,128)(2,1)}, u32[]{:S(2)}, u32[]{:S(2)}) collective-permute-start(bf16[416,384]{1,0:T(8,128)(2,1)S(1)} %collective-permute-done.10.refs_1_), channel_id=1, source_target_pairs={{0,1},{1,0},{2,3},{3,2},{4,5},{5,4},{6,7},{7,6},{8,9},{9,8},{10,11... | collective-permute-start | bytes 958472 | tf_op jit(solution)/shard_map/ppermute | solution.py:85
  58.9 5.4 %collective-permute-start.17 = (bf16[768,384]{1,0:T(8,128)(2,1)S(1)}, bf16[768,384]{1,0:T(8,128)(2,1)}, u32[]{:S(2)}, u32[]{:S(2)}) collective-permute-start(bf16[768,384]{1,0:T(8,128)(2,1)S(1)} %second_merge_x.1.refs_0_), channel_id=1, source_target_pairs={{0,1},{1,0},{2,3},{3,2},{4,5},{5,4},{6,7},{7,6},{8,9},{9,8},{10,11... | collective-permute-start | bytes 1769480 | tf_op jit(solution)/shard_map/ppermute | solution.py:85
  66.9 13.8 %collective-permute-start.23 = (bf16[1152,384]{1,0:T(8,128)(2,1)S(1)}, bf16[1152,384]{1,0:T(8,128)(2,1)}, u32[]{:S(2)}, u32[]{:S(2)}) collective-permute-start(bf16[1152,384]{1,0:T(8,128)(2,1)S(1)} %third_merge_x.1.refs_0_), channel_id=1, source_target_pairs={{0,1},{1,0},{2,3},{3,2},{4,5},{5,4},{6,7},{7,6},{8,9},{9,8},{10,11... | collective-permute-start | bytes 2654216 | tf_op jit(solution)/shard_map/ppermute | solution.py:85
  84.1 3.5 %fusion.32.q_ref.k_ref.v_ref = bf16[577,1152]{1,0:T(8,128)(2,1)} fusion(bf16[1152,384]{1,0:T(8,128)(2,1)} %copy-done.17, f32[1152]{0:T(1024)S(1)} %get-tuple-element.229, f32[384]{0:T(512)S(1)} %get-tuple-element.186, f32[384]{0:T(512)S(1)} %get-tuple-element.187, f32[1,577,384]{2,0,1:T(1,128)} %param.9, f32[577]{0:T(1024)S(1)} %add_rsqrt_fusion.3, ...), kind=kOutput, calls=%fused_computation.58 | convolution fusion | flops 512929920 | bytes 3112712 | tf_op jit(solution)/shard_map/dot_general | solution.py:63
  89.2 5.8 %attend.2 = (bf16[577,384]{1,0:T(8,128)(2,1)S(1)}, bf16[6,577,577]{2,1,0:T(8,128)(2,1)S(1)}) custom-call(bf16[577,1152]{1,0:T(8,128)(2,1)S(1)} %copy-done.19, bf16[577,1152]{1,0:T(8,128)(2,1)S(1)} %copy-done.19, bf16[577,1152]{1,0:T(8,128)(2,1)S(1)} %copy-done.19), custom_call_target="tpu_custom_call" | custom-call | flops 2045515776 | bytes 5767692 | tf_op jit(solution)/shard_map/attend/pallas_call | solution.py:493
  101.4 8.3 %fusion.2 = (bf16[577,1536]{1,0:T(8,128)(2,1)S(1)}, f32[577,1536]{1,0:T(8,128)S(1)}) fusion(f32[1536]{0:T(1024)S(1)} %add.220, bf16[1536,384]{1,0:T(8,128)(2,1)S(1)} %get-tuple-element.84, f32[577,384]{1,0:T(8,128)S(1)} %get-tuple-element.231, f32[384]{0:T(512)S(1)} %get-tuple-element.181, f32[384]{0:T(512)S(1)} %get-tuple-element.182, ...), kind=kOutput, calls=%fused_computation.8 | convolution fusion | flops 740258688 | bytes 7397384 | tf_op jit(solution)/shard_map/dot_general | solution.py:63
  114.8 6.2 %attend.3 = (bf16[577,384]{1,0:T(8,128)(2,1)S(1)}, bf16[6,577,577]{2,1,0:T(8,128)(2,1)S(1)}) custom-call(bf16[577,1152]{1,0:T(8,128)(2,1)S(1)} %fusion.33.q_ref.k_ref.v_ref, bf16[577,1152]{1,0:T(8,128)(2,1)S(1)} %fusion.33.q_ref.k_ref.v_ref, bf16[577,1152]{1,0:T(8,128)(2,1)S(1)} %fusion.33.q_ref.k_ref.v_ref), custom_call_target="tpu_custom_call" | custom-call | flops 2045515776 | bytes 5767692 | tf_op jit(solution)/shard_map/attend/pallas_call | solution.py:493
  121.9 8.4 %fusion.5 = (bf16[577,1536]{1,0:T(8,128)(2,1)S(1)}, f32[577,1536]{1,0:T(8,128)S(1)}) fusion(f32[1536]{0:T(1024)S(1)} %add.241, bf16[1536,384]{1,0:T(8,128)(2,1)S(1)} %get-tuple-element.90, f32[577,384]{1,0:T(8,128)S(1)} %get-tuple-element.237, f32[384]{0:T(512)S(1)} %get-tuple-element.173, f32[384]{0:T(512)S(1)} %get-tuple-element.174, ...), kind=kOutput, calls=%fused_computation.11 | convolution fusion | flops 740258688 | bytes 7397384 | tf_op jit(solution)/shard_map/dot_general | solution.py:63
  130.3 2.7 convert_reduce_fusion
  137.4 7.7 %attend_back.2 = bf16[577,1152]{1,0:T(8,128)(2,1)S(1)} custom-call(bf16[577,1152]{1,0:T(8,128)(2,1)S(1)} %fusion.33.q_ref.k_ref.v_ref, bf16[577,1152]{1,0:T(8,128)(2,1)S(1)} %fusion.33.q_ref.k_ref.v_ref, bf16[577,1152]{1,0:T(8,128)(2,1)S(1)} %fusion.33.q_ref.k_ref.v_ref, bf16[577,384]{1,0:T(8,128)(2,1)S(1)} %convolution_convert_fusion.7.up_ref, ...), custom_call_target="tpu_custom_call" | custom-call | flops 4091031552 | bytes 7540236 | tf_op jit(solution)/shard_map/attend_back/pallas_call | solution.py:546
  150.9 3.4 %convert_reduce_fusion.1 = (f32[1536]{0:T(1024)S(1)}, bf16[577,1536]{1,0:T(8,128)(2,1)}) fusion(f32[577,1536]{1,0:T(8,128)S(1)} %get-tuple-element.233, bf16[1536,384]{1,0:T(8,128)(2,1)S(1)} %get-tuple-element.85, f32[577,384]{1,0:T(8,128)S(1)} %multiply_add_fusion.1), kind=kOutput, calls=%fused_computation.25 | convolution fusion | flops 691512192 | bytes 7389696 | tf_op jit(solution)/shard_map/dot_general | solution.py:63
  155.1 3.8 %multiply_reduce_fusion.2 = (f32[384]{0:T(512)S(1)}, f32[577]{0:T(1024)S(1)}, f32[577]{0:T(1024)S(1)}, f32[384]{0:T(512)S(1)}, f32[577,384]{1,0:T(8,128)}) fusion(f32[577,384]{1,0:T(8,128)} %copy-done.28, f32[577]{0:T(1024)S(1)} %add_rsqrt_fusion.2, f32[577]{0:T(1024)S(1)} %broadcast_multiply_fusion.10, f32[384]{0:T(512)S(1)} %get-tuple-element.182, ...), kind=kOutput, calls=%fused_computation.90 | convolution fusion | flops 682649088 | bytes 4738576 | tf_op jit(solution)/shard_map/dot_general | solution.py:593
  170.9 7.7 %attend_back.3 = bf16[577,1152]{1,0:T(8,128)(2,1)S(1)} custom-call(bf16[577,1152]{1,0:T(8,128)(2,1)S(1)} %copy-done.20, bf16[577,1152]{1,0:T(8,128)(2,1)S(1)} %copy-done.20, bf16[577,1152]{1,0:T(8,128)(2,1)S(1)} %copy-done.20, bf16[577,384]{1,0:T(8,128)(2,1)S(1)} %convolution_convert_fusion.6.up_ref, bf16[6,577,577]{2,1,0:T(8,128)(2,1)S(1)} %bitcast.93), custom_call_target="tpu_custom_call" | custom-call | flops 4091031552 | bytes 7540236 | tf_op jit(solution)/shard_map/attend_back/pallas_call | solution.py:546
  190.6 12.8 %collective-permute-done.31.refs_1_ = bf16[1152,384]{1,0:T(8,128)(2,1)} collective-permute-done((bf16[1152,384]{1,0:T(8,128)(2,1)}, bf16[1152,384]{1,0:T(8,128)(2,1)}, u32[]{:S(2)}, u32[]{:S(2)}) %collective-permute-start.31) | collective-permute-done | bytes 884768 | tf_op jit(solution)/shard_map/ppermute | solution.py:85
  208.4 7.5 %collective-permute-done.27.refs_1_ = bf16[768,384]{1,0:T(8,128)(2,1)S(1)} collective-permute-done((bf16[768,384]{1,0:T(8,128)(2,1)S(1)}, bf16[768,384]{1,0:T(8,128)(2,1)S(1)}, u32[]{:S(2)}, u32[]{:S(2)}) %collective-permute-start.27) | collective-permute-done | bytes 589856 | tf_op jit(solution)/shard_map/ppermute | solution.py:85
  216.1 7.2 %collective-permute-done.36.refs_1_ = bf16[448,384]{1,0:T(8,128)(2,1)S(1)} collective-permute-done((bf16[448,384]{1,0:T(8,128)(2,1)S(1)}, bf16[448,384]{1,0:T(8,128)(2,1)S(1)}, u32[]{:S(2)}, u32[]{:S(2)}) %collective-permute-start.36) | collective-permute-done | bytes 344096 | tf_op jit(solution)/shard_map/ppermute | solution.py:85
  229.5 6.9 %collective-permute-done.29.refs_2_ = bf16[192,384]{1,0:T(8,128)(2,1)S(1)} collective-permute-done((bf16[192,384]{1,0:T(8,128)(2,1)S(1)}, bf16[192,384]{1,0:T(8,128)(2,1)S(1)}, u32[]{:S(2)}, u32[]{:S(2)}) %collective-permute-start.29) | collective-permute-done | bytes 147488 | tf_op jit(solution)/shard_map/ppermute | solution.py:85
  236.4 5.3 %collective-permute-done.30.refs_3_ = bf16[192,384]{1,0:T(8,128)(2,1)S(1)} collective-permute-done((bf16[192,384]{1,0:T(8,128)(2,1)S(1)}, bf16[192,384]{1,0:T(8,128)(2,1)S(1)}, u32[]{:S(2)}, u32[]{:S(2)}) %collective-permute-start.30) | collective-permute-done | bytes 147488 | tf_op jit(solution)/shard_map/ppermute | solution.py:85
  242.6 2.9 collective-permute-start.40
  249.7 2.7 collective-permute-start.45
  252.5 3.2 %collective-permute-start.46 = (bf16[160,384]{1,0:T(8,128)(2,1)S(1)}, bf16[160,384]{1,0:T(8,128)(2,1)S(1)}, u32[]{:S(2)}, u32[]{:S(2)}) collective-permute-start(bf16[160,384]{1,0:T(8,128)(2,1)S(1)} %get-tuple-element.134), channel_id=1, source_target_pairs={{0,112},{16,64},{32,80},{48,96},{64,48},{80,0},{96,16},{112,32},{1... | collective-permute-start | bytes 368648 | tf_op jit(solution)/shard_map/ppermute | solution.py:102
  255.7 2.9 collective-permute-done.45.refs_5_
  261.8 3.1 %collective-permute-start.47 = (bf16[96,384]{1,0:T(8,128)(2,1)S(1)}, bf16[96,384]{1,0:T(8,128)(2,1)S(1)}, u32[]{:S(2)}, u32[]{:S(2)}) collective-permute-start(bf16[96,384]{1,0:T(8,128)(2,1)S(1)} %get-tuple-element.138.refs_4_), channel_id=1, source_target_pairs={{0,12},{1,13},{2,14},{3,15},{4,0},{5,1},{6,2},{7,3},{8,4},{9,5},{1... | collective-permute-start | bytes 221192 | tf_op jit(solution)/shard_map/ppermute | solution.py:85
  271.5 4.5 %collective-permute-start.51 = (bf16[384,384]{1,0:T(8,128)(2,1)S(1)}, bf16[384,384]{1,0:T(8,128)(2,1)S(1)}, u32[]{:S(2)}, u32[]{:S(2)}) collective-permute-start(bf16[384,384]{1,0:T(8,128)(2,1)S(1)} %constant_dynamic-update-slice_fusion.refs_0_), channel_id=1, source_target_pairs={{0,1},{1,0},{2,3},{3,2},{4,5},{5,4},{6,7},{7,6},{8,9},{9,8},{10,11... | collective-permute-start | bytes 884744 | tf_op jit(solution)/shard_map/ppermute | solution.py:85
  276.0 5.3 %collective-permute-start.52 = (bf16[384,384]{1,0:T(8,128)(2,1)S(1)}, bf16[384,384]{1,0:T(8,128)(2,1)S(1)}, u32[]{:S(2)}, u32[]{:S(2)}) collective-permute-start(bf16[384,384]{1,0:T(8,128)(2,1)S(1)} %collective-permute-done.50.refs_1_), channel_id=1, source_target_pairs={{0,1},{1,0},{2,3},{3,2},{4,5},{5,4},{6,7},{7,6},{8,9},{9,8},{10,11... | collective-permute-start | bytes 884744 | tf_op jit(solution)/shard_map/ppermute | solution.py:85
  286.8 13.7 %newton.1 = f32[96,384]{1,0:T(8,128)} custom-call(s32[8]{0:T(128)S(1)} %copy-done.11, bf16[384,384]{1,0:T(8,128)(2,1)S(1)} %constant_dynamic-update-slice_fusion.refs_0_, bf16[384,384]{1,0:T(8,128)(2,1)S(1)} %collective-permute-done.50.refs_1_, bf16[384,384]{1,0:T(8,128)(2,1)S(1)} %collective-permute-done.51.refs_2_, ...), custom_call_target="tpu_custom_call" | custom-call | tf_op jit(solution)/shard_map/newton/pallas_call | solution.py:123
  (309 shorter events, 114.6 us)
Async XLA Ops:
  2.8 10.0 %collective-permute-start = (bf16[128,384]{1,0:T(8,128)(2,1)S(1)}, bf16[128,384]{1,0:T(8,128)(2,1)S(1)}, u32[]{:S(2)}, u32[]{:S(2)}) collective-permute-start(bf16[128,384]{1,0:T(8,128)(2,1)S(1)} %pad_maximum_fusion.refs_0_), channel_id=1, source_target_pairs={{0,48},{16,0},{32,16},{48,32},{64,112},{80,64},{96,80},{112,96},{1... | collective-permute-start | bytes 294920 | tf_op jit(solution)/shard_map/ppermute | solution.py:102
  7.5 9.8 %collective-permute-start.1 = (bf16[128,384]{1,0:T(8,128)(2,1)S(1)}, bf16[128,384]{1,0:T(8,128)(2,1)S(1)}, u32[]{:S(2)}, u32[]{:S(2)}) collective-permute-start(bf16[128,384]{1,0:T(8,128)(2,1)S(1)} %pad_maximum_fusion.refs_0_), channel_id=1, source_target_pairs={{0,32},{16,48},{32,0},{48,16},{64,96},{80,112},{96,64},{112,80},{1... | collective-permute-start | bytes 294920 | tf_op jit(solution)/shard_map/ppermute | solution.py:102
  7.5 10.6 %collective-permute-start.2 = (bf16[128,384]{1,0:T(8,128)(2,1)S(1)}, bf16[128,384]{1,0:T(8,128)(2,1)S(1)}, u32[]{:S(2)}, u32[]{:S(2)}) collective-permute-start(bf16[128,384]{1,0:T(8,128)(2,1)S(1)} %pad_maximum_fusion.refs_0_), channel_id=1, source_target_pairs={{0,16},{16,32},{32,48},{48,0},{64,80},{80,96},{96,112},{112,64},{1... | collective-permute-start | bytes 294920 | tf_op jit(solution)/shard_map/ppermute | solution.py:102
  8.2 9.9 %collective-permute-start.3 = (bf16[128,384]{1,0:T(8,128)(2,1)S(1)}, bf16[128,384]{1,0:T(8,128)(2,1)S(1)}, u32[]{:S(2)}, u32[]{:S(2)}) collective-permute-start(bf16[128,384]{1,0:T(8,128)(2,1)S(1)} %pad_maximum_fusion.refs_0_), channel_id=1, source_target_pairs={{0,64},{16,80},{32,96},{48,112},{64,0},{80,16},{96,32},{112,48},{1... | collective-permute-start | bytes 294920 | tf_op jit(solution)/shard_map/ppermute | solution.py:102
  35.8 15.3 %collective-permute-start.10 = (bf16[416,384]{1,0:T(8,128)(2,1)S(1)}, bf16[416,384]{1,0:T(8,128)(2,1)S(1)}, u32[]{:S(2)}, u32[]{:S(2)}) collective-permute-start(bf16[416,384]{1,0:T(8,128)(2,1)S(1)} %first_merge_x.1.refs_0_), channel_id=1, source_target_pairs={{0,2},{1,3},{2,0},{3,1},{4,6},{5,7},{6,4},{7,5},{8,10},{9,11},{10,... | collective-permute-start | bytes 958472 | tf_op jit(solution)/shard_map/ppermute | solution.py:85
  41.4 24.9 %collective-permute-start.11 = (bf16[416,384]{1,0:T(8,128)(2,1)S(1)}, bf16[416,384]{1,0:T(8,128)(2,1)S(1)}, u32[]{:S(2)}, u32[]{:S(2)}) collective-permute-start(bf16[416,384]{1,0:T(8,128)(2,1)S(1)} %first_merge_x.1.refs_0_), channel_id=1, source_target_pairs={{0,1},{1,0},{2,3},{3,2},{4,5},{5,4},{6,7},{7,6},{8,9},{9,8},{10,11... | collective-permute-start | bytes 958472 | tf_op jit(solution)/shard_map/ppermute | solution.py:85
  47.3 10.2 %collective-permute-start.19 = (bf16[384,384]{1,0:T(8,128)(2,1)S(1)}, bf16[384,384]{1,0:T(8,128)(2,1)S(1)}, u32[]{:S(2)}, u32[]{:S(2)}) collective-permute-start(bf16[384,384]{1,0:T(8,128)(2,1)S(1)} %get-tuple-element.86.refs_0_), channel_id=1, source_target_pairs={{0,12},{1,13},{2,14},{3,15},{4,0},{5,1},{6,2},{7,3},{8,4},{9,5},{1... | collective-permute-start | bytes 884744 | tf_op jit(solution)/shard_map/ppermute | solution.py:85
  48.8 10.1 %collective-permute-start.20 = (bf16[384,384]{1,0:T(8,128)(2,1)S(1)}, bf16[384,384]{1,0:T(8,128)(2,1)S(1)}, u32[]{:S(2)}, u32[]{:S(2)}) collective-permute-start(bf16[384,384]{1,0:T(8,128)(2,1)S(1)} %get-tuple-element.86.refs_0_), channel_id=1, source_target_pairs={{0,8},{1,9},{2,10},{3,11},{4,12},{5,13},{6,14},{7,15},{8,0},{9,1},... | collective-permute-start | bytes 884744 | tf_op jit(solution)/shard_map/ppermute | solution.py:85
  50.4 13.9 %collective-permute-start.21 = (bf16[384,384]{1,0:T(8,128)(2,1)S(1)}, bf16[384,384]{1,0:T(8,128)(2,1)S(1)}, u32[]{:S(2)}, u32[]{:S(2)}) collective-permute-start(bf16[384,384]{1,0:T(8,128)(2,1)S(1)} %get-tuple-element.86.refs_0_), channel_id=1, source_target_pairs={{0,4},{1,5},{2,6},{3,7},{4,8},{5,9},{6,10},{7,11},{8,12},{9,13},{1... | collective-permute-start | bytes 884744 | tf_op jit(solution)/shard_map/ppermute | solution.py:85
  51.1 29.6 %collective-permute-start.12 = (bf16[416,384]{1,0:T(8,128)(2,1)S(1)}, bf16[416,384]{1,0:T(8,128)(2,1)}, u32[]{:S(2)}, u32[]{:S(2)}) collective-permute-start(bf16[416,384]{1,0:T(8,128)(2,1)S(1)} %collective-permute-done.10.refs_1_), channel_id=1, source_target_pairs={{0,1},{1,0},{2,3},{3,2},{4,5},{5,4},{6,7},{7,6},{8,9},{9,8},{10,11... | collective-permute-start | bytes 958472 | tf_op jit(solution)/shard_map/ppermute | solution.py:85
  57.5 40.1 %collective-permute-start.16 = (bf16[768,384]{1,0:T(8,128)(2,1)S(1)}, bf16[768,384]{1,0:T(8,128)(2,1)}, u32[]{:S(2)}, u32[]{:S(2)}) collective-permute-start(bf16[768,384]{1,0:T(8,128)(2,1)S(1)} %second_merge_x.1.refs_0_), channel_id=1, source_target_pairs={{0,2},{1,3},{2,0},{3,1},{4,6},{5,7},{6,4},{7,5},{8,10},{9,11},{10,... | collective-permute-start | bytes 1769480 | tf_op jit(solution)/shard_map/ppermute | solution.py:85
  58.9 39.1 %collective-permute-start.17 = (bf16[768,384]{1,0:T(8,128)(2,1)S(1)}, bf16[768,384]{1,0:T(8,128)(2,1)}, u32[]{:S(2)}, u32[]{:S(2)}) collective-permute-start(bf16[768,384]{1,0:T(8,128)(2,1)S(1)} %second_merge_x.1.refs_0_), channel_id=1, source_target_pairs={{0,1},{1,0},{2,3},{3,2},{4,5},{5,4},{6,7},{7,6},{8,9},{9,8},{10,11... | collective-permute-start | bytes 1769480 | tf_op jit(solution)/shard_map/ppermute | solution.py:85
  66.1 43.7 %collective-permute-start.22 = (bf16[1152,384]{1,0:T(8,128)(2,1)S(1)}, bf16[1152,384]{1,0:T(8,128)(2,1)S(1)}, u32[]{:S(2)}, u32[]{:S(2)}) collective-permute-start(bf16[1152,384]{1,0:T(8,128)(2,1)S(1)} %third_merge_x.1.refs_0_), channel_id=1, source_target_pairs={{0,2},{1,3},{2,0},{3,1},{4,6},{5,7},{6,4},{7,5},{8,10},{9,11},{10,... | collective-permute-start | bytes 2654216 | tf_op jit(solution)/shard_map/ppermute | solution.py:85
  66.9 44.6 %collective-permute-start.23 = (bf16[1152,384]{1,0:T(8,128)(2,1)S(1)}, bf16[1152,384]{1,0:T(8,128)(2,1)}, u32[]{:S(2)}, u32[]{:S(2)}) collective-permute-start(bf16[1152,384]{1,0:T(8,128)(2,1)S(1)} %third_merge_x.1.refs_0_), channel_id=1, source_target_pairs={{0,1},{1,0},{2,3},{3,2},{4,5},{5,4},{6,7},{7,6},{8,9},{9,8},{10,11... | collective-permute-start | bytes 2654216 | tf_op jit(solution)/shard_map/ppermute | solution.py:85
  154.7 11.7 %collective-permute-start.25 = (bf16[2304,384]{1,0:T(8,128)(2,1)}, bf16[2304,384]{1,0:T(8,128)(2,1)}, u32[]{:S(2)}, u32[]{:S(2)}) collective-permute-start(bf16[2304,384]{1,0:T(8,128)(2,1)} %copy-done.12), channel_id=1, source_target_pairs={{0,1},{1,0},{2,3},{3,2},{4,5},{5,4},{6,7},{7,6},{8,9},{9,8},{10,11... | collective-permute-start | bytes 5308424 | tf_op jit(solution)/shard_map/ppermute | solution.py:85
  181.9 21.5 %collective-permute-start.31 = (bf16[1152,384]{1,0:T(8,128)(2,1)}, bf16[1152,384]{1,0:T(8,128)(2,1)}, u32[]{:S(2)}, u32[]{:S(2)}) collective-permute-start(bf16[1152,384]{1,0:T(8,128)(2,1)} %get-tuple-element.112), channel_id=1, source_target_pairs={{0,2},{1,3},{2,0},{3,1},{4,6},{5,7},{6,4},{7,5},{8,10},{9,11},{10,... | collective-permute-start | bytes 2654216 | tf_op jit(solution)/shard_map/ppermute | solution.py:85
  187.7 28.3 %collective-permute-start.27 = (bf16[768,384]{1,0:T(8,128)(2,1)S(1)}, bf16[768,384]{1,0:T(8,128)(2,1)S(1)}, u32[]{:S(2)}, u32[]{:S(2)}) collective-permute-start(bf16[768,384]{1,0:T(8,128)(2,1)S(1)} %get-tuple-element.106), channel_id=1, source_target_pairs={{0,2},{1,3},{2,0},{3,1},{4,6},{5,7},{6,4},{7,5},{8,10},{9,11},{10,... | collective-permute-start | bytes 1769480 | tf_op jit(solution)/shard_map/ppermute | solution.py:85
  189.5 33.8 %collective-permute-start.36 = (bf16[448,384]{1,0:T(8,128)(2,1)S(1)}, bf16[448,384]{1,0:T(8,128)(2,1)S(1)}, u32[]{:S(2)}, u32[]{:S(2)}) collective-permute-start(bf16[448,384]{1,0:T(8,128)(2,1)S(1)} %get-tuple-element.120), channel_id=1, source_target_pairs={{0,2},{1,3},{2,0},{3,1},{4,6},{5,7},{6,4},{7,5},{8,10},{9,11},{10,... | collective-permute-start | bytes 1032200 | tf_op jit(solution)/shard_map/ppermute | solution.py:85
  204.9 18.6 %collective-permute-start.32 = (bf16[384,384]{1,0:T(8,128)(2,1)S(1)}, bf16[384,384]{1,0:T(8,128)(2,1)S(1)}, u32[]{:S(2)}, u32[]{:S(2)}) collective-permute-start(bf16[384,384]{1,0:T(8,128)(2,1)S(1)} %get-tuple-element.114), channel_id=1, source_target_pairs={{0,4},{1,5},{2,6},{3,7},{4,8},{5,9},{6,10},{7,11},{8,12},{9,13},{1... | collective-permute-start | bytes 884744 | tf_op jit(solution)/shard_map/ppermute | solution.py:85
  205.0 20.1 %collective-permute-start.33 = (bf16[384,384]{1,0:T(8,128)(2,1)S(1)}, bf16[384,384]{1,0:T(8,128)(2,1)S(1)}, u32[]{:S(2)}, u32[]{:S(2)}) collective-permute-start(bf16[384,384]{1,0:T(8,128)(2,1)S(1)} %get-tuple-element.115), channel_id=1, source_target_pairs={{0,8},{1,9},{2,10},{3,11},{4,12},{5,13},{6,14},{7,15},{8,0},{9,1},... | collective-permute-start | bytes 884744 | tf_op jit(solution)/shard_map/ppermute | solution.py:85
  206.6 20.4 %collective-permute-start.34 = (bf16[384,384]{1,0:T(8,128)(2,1)S(1)}, bf16[384,384]{1,0:T(8,128)(2,1)S(1)}, u32[]{:S(2)}, u32[]{:S(2)}) collective-permute-start(bf16[384,384]{1,0:T(8,128)(2,1)S(1)} %get-tuple-element.116), channel_id=1, source_target_pairs={{0,12},{1,13},{2,14},{3,15},{4,0},{5,1},{6,2},{7,3},{8,4},{9,5},{1... | collective-permute-start | bytes 884744 | tf_op jit(solution)/shard_map/ppermute | solution.py:85
  216.0 12.6 %collective-permute-start.28 = (bf16[192,384]{1,0:T(8,128)(2,1)S(1)}, bf16[192,384]{1,0:T(8,128)(2,1)S(1)}, u32[]{:S(2)}, u32[]{:S(2)}) collective-permute-start(bf16[192,384]{1,0:T(8,128)(2,1)S(1)} %get-tuple-element.108), channel_id=1, source_target_pairs={{0,4},{1,5},{2,6},{3,7},{4,8},{5,9},{6,10},{7,11},{8,12},{9,13},{1... | collective-permute-start | bytes 442376 | tf_op jit(solution)/shard_map/ppermute | solution.py:85
  223.5 18.3 %collective-permute-start.37 = (bf16[256,384]{1,0:T(8,128)(2,1)S(1)}, bf16[256,384]{1,0:T(8,128)(2,1)S(1)}, u32[]{:S(2)}, u32[]{:S(2)}) collective-permute-start(bf16[256,384]{1,0:T(8,128)(2,1)S(1)} %get-tuple-element.123), channel_id=1, source_target_pairs={{0,4},{1,5},{2,6},{3,7},{4,8},{5,9},{6,10},{7,11},{8,12},{9,13},{1... | collective-permute-start | bytes 589832 | tf_op jit(solution)/shard_map/ppermute | solution.py:85
  223.6 18.2 %collective-permute-start.38 = (bf16[256,384]{1,0:T(8,128)(2,1)S(1)}, bf16[256,384]{1,0:T(8,128)(2,1)S(1)}, u32[]{:S(2)}, u32[]{:S(2)}) collective-permute-start(bf16[256,384]{1,0:T(8,128)(2,1)S(1)} %get-tuple-element.124), channel_id=1, source_target_pairs={{0,8},{1,9},{2,10},{3,11},{4,12},{5,13},{6,14},{7,15},{8,0},{9,1},... | collective-permute-start | bytes 589832 | tf_op jit(solution)/shard_map/ppermute | solution.py:85
  225.1 16.7 %collective-permute-start.39 = (bf16[256,384]{1,0:T(8,128)(2,1)S(1)}, bf16[256,384]{1,0:T(8,128)(2,1)S(1)}, u32[]{:S(2)}, u32[]{:S(2)}) collective-permute-start(bf16[256,384]{1,0:T(8,128)(2,1)S(1)} %get-tuple-element.125), channel_id=1, source_target_pairs={{0,12},{1,13},{2,14},{3,15},{4,0},{5,1},{6,2},{7,3},{8,4},{9,5},{1... | collective-permute-start | bytes 589832 | tf_op jit(solution)/shard_map/ppermute | solution.py:85
  227.0 9.4 %collective-permute-start.29 = (bf16[192,384]{1,0:T(8,128)(2,1)S(1)}, bf16[192,384]{1,0:T(8,128)(2,1)S(1)}, u32[]{:S(2)}, u32[]{:S(2)}) collective-permute-start(bf16[192,384]{1,0:T(8,128)(2,1)S(1)} %get-tuple-element.109), channel_id=1, source_target_pairs={{0,8},{1,9},{2,10},{3,11},{4,12},{5,13},{6,14},{7,15},{8,0},{9,1},... | collective-permute-start | bytes 442376 | tf_op jit(solution)/shard_map/ppermute | solution.py:85
  228.6 13.1 %collective-permute-start.30 = (bf16[192,384]{1,0:T(8,128)(2,1)S(1)}, bf16[192,384]{1,0:T(8,128)(2,1)S(1)}, u32[]{:S(2)}, u32[]{:S(2)}) collective-permute-start(bf16[192,384]{1,0:T(8,128)(2,1)S(1)} %get-tuple-element.110), channel_id=1, source_target_pairs={{0,12},{1,13},{2,14},{3,15},{4,0},{5,1},{6,2},{7,3},{8,4},{9,5},{1... | collective-permute-start | bytes 442376 | tf_op jit(solution)/shard_map/ppermute | solution.py:85
  245.6 10.1 %collective-permute-start.42 = (bf16[160,384]{1,0:T(8,128)(2,1)S(1)}, bf16[160,384]{1,0:T(8,128)(2,1)S(1)}, u32[]{:S(2)}, u32[]{:S(2)}) collective-permute-start(bf16[160,384]{1,0:T(8,128)(2,1)S(1)} %get-tuple-element.130), channel_id=1, source_target_pairs={{0,48},{16,0},{32,16},{48,32},{64,112},{80,64},{96,80},{112,96},{1... | collective-permute-start | bytes 368648 | tf_op jit(solution)/shard_map/ppermute | solution.py:102
  249.7 8.9 %collective-permute-start.45 = (bf16[160,384]{1,0:T(8,128)(2,1)S(1)}, bf16[160,384]{1,0:T(8,128)(2,1)S(1)}, u32[]{:S(2)}, u32[]{:S(2)}) collective-permute-start(bf16[160,384]{1,0:T(8,128)(2,1)S(1)} %get-tuple-element.133), channel_id=1, source_target_pairs={{0,96},{16,112},{32,64},{48,80},{64,32},{80,48},{96,0},{112,16},{1... | collective-permute-start | bytes 368648 | tf_op jit(solution)/shard_map/ppermute | solution.py:102
  252.5 8.5 %collective-permute-start.46 = (bf16[160,384]{1,0:T(8,128)(2,1)S(1)}, bf16[160,384]{1,0:T(8,128)(2,1)S(1)}, u32[]{:S(2)}, u32[]{:S(2)}) collective-permute-start(bf16[160,384]{1,0:T(8,128)(2,1)S(1)} %get-tuple-element.134), channel_id=1, source_target_pairs={{0,112},{16,64},{32,80},{48,96},{64,48},{80,0},{96,16},{112,32},{1... | collective-permute-start | bytes 368648 | tf_op jit(solution)/shard_map/ppermute | solution.py:102
  271.5 15.3 %collective-permute-start.51 = (bf16[384,384]{1,0:T(8,128)(2,1)S(1)}, bf16[384,384]{1,0:T(8,128)(2,1)S(1)}, u32[]{:S(2)}, u32[]{:S(2)}) collective-permute-start(bf16[384,384]{1,0:T(8,128)(2,1)S(1)} %constant_dynamic-update-slice_fusion.refs_0_), channel_id=1, source_target_pairs={{0,1},{1,0},{2,3},{3,2},{4,5},{5,4},{6,7},{7,6},{8,9},{9,8},{10,11... | collective-permute-start | bytes 884744 | tf_op jit(solution)/shard_map/ppermute | solution.py:85
  276.0 10.8 %collective-permute-start.52 = (bf16[384,384]{1,0:T(8,128)(2,1)S(1)}, bf16[384,384]{1,0:T(8,128)(2,1)S(1)}, u32[]{:S(2)}, u32[]{:S(2)}) collective-permute-start(bf16[384,384]{1,0:T(8,128)(2,1)S(1)} %collective-permute-done.50.refs_1_), channel_id=1, source_target_pairs={{0,1},{1,0},{2,3},{3,2},{4,5},{5,4},{6,7},{7,6},{8,9},{9,8},{10,11... | collective-permute-start | bytes 884744 | tf_op jit(solution)/shard_map/ppermute | solution.py:85
  (65 other events, 599.5 us)
